TPU v7x, 512 devices: a whole 4x4x16 slice. The times are simulated.
512 devices in a mesh: ex: 32 (over z, x_hi), par: 16 (over y, x_lo, core).
Axes of the slice: x: 4 (x_hi: 2, x_lo: 2; x = x_hi * 2 + x_lo), y: 4, z: 16, core: 2. Of those that a mesh axis runs over, the one named last changes fastest.
Arguments:
- jacobian: bfloat16 [2560, 131072], P('ex', 'par'), may hold values from -0.29882812 to 0.29882812
Outputs:
- gram: float32 [2560, 2560], P('ex', 'par')
All inputs are finite; a program needn't handle non-finite values.
Results may differ from a plain program's by a relative error of at most 0.0035.
Values may be sent and summed in bfloat16 or wider, within the bound.
No kernel may reach another device: no remote copies, remote signals or barrier semaphores. Data moves between devices by JAX's collectives and lax.ppermute only.
A program may use at most 64 MiB of HBM per device.

v0:
```python
import jax
import jax.numpy as jnp
from jax import lax
from jax.sharding import PartitionSpec as P


def partner_2(value, axis, distance):
    mask = 2**distance
    pairs = [(source, source ^ mask) for source in range(lax.axis_size(axis))]
    return lax.ppermute(value, axis, pairs)


def from_behind(block, axis, distance):
    devices = range(lax.axis_size(axis))
    route = [((i - distance) % len(devices), i) for i in devices]
    return lax.ppermute(block, axis, route)


def tile_of(rows_a, rows_b):
    return lax.dot_general(
        rows_a, rows_b, (((1,), (1,)), ((), ())), preferred_element_type=jnp.float32
    )


def put_tile(tile_stack, tile_value, column):
    return lax.dynamic_update_slice_in_dim(tile_stack, tile_value[None], column, 0)


def shards(jacobian):
    ex_size = lax.axis_size("ex")
    groups = ex_size // 2
    half_groups = groups // 2
    position = lax.axis_index("ex")
    group = position // 2
    member = position % 2
    row_count, col_count = jacobian.shape
    pair_cols = col_count // 2
    outgoing = lax.dynamic_slice_in_dim(jacobian, (1 - member) * pair_cols, pair_cols, 1)
    partner = partner_2(outgoing, "ex", 0)
    mine = lax.dynamic_slice_in_dim(jacobian, member * pair_cols, pair_cols, 1)
    pair_block = jnp.where(
        member == 0, jnp.concatenate([mine, partner], 0), jnp.concatenate([partner, mine], 0)
    )
    block_rows = 2 * row_count
    own_tiles = jnp.zeros((groups, block_rows, block_rows), jnp.float32)
    mirror = jnp.zeros((groups, block_rows, block_rows), jnp.float32)
    own_tiles = put_tile(own_tiles, tile_of(pair_block, pair_block), group)
    tile_state = (own_tiles, mirror)
    travel_block = pair_block
    for distance in range(1, half_groups):
        travel_block = from_behind(travel_block, "ex", -2)
        column = group + distance
        tiles_now, mirror_now = tile_state
        tile_value = tile_of(pair_block, travel_block)
        column = jnp.mod(column, groups)
        tile_state = (
            put_tile(tiles_now, tile_value, column),
            put_tile(mirror_now, tile_value.T, column),
        )
    quarter_cols = pair_cols // 2
    side = group // half_groups
    leaving = lax.dynamic_slice_in_dim(pair_block, (1 - side) * quarter_cols, quarter_cols, 1)
    incoming = from_behind(leaving, "ex", ex_size // 2)
    own_quarter = lax.dynamic_slice_in_dim(pair_block, side * quarter_cols, quarter_cols, 1)
    half_tile = tile_of(own_quarter, incoming)
    opposite = jnp.mod(group + half_groups, groups)
    own_tiles, mirror = tile_state
    own_tiles = put_tile(own_tiles, half_tile, opposite)
    mirror = put_tile(mirror, half_tile.T, opposite)
    keep = lax.dynamic_slice_in_dim(own_tiles, member * row_count, row_count, 1)
    give = lax.dynamic_slice_in_dim(own_tiles, (1 - member) * row_count, row_count, 1)
    mirror_rows = mirror.reshape(ex_size, row_count, block_rows)
    given = partner_2(give.astype(jnp.bfloat16), "ex", 0).astype(give.dtype)
    returned = lax.all_to_all(
        mirror_rows.astype(jnp.bfloat16), "ex", split_axis=0, concat_axis=0, tiled=True
    ).astype(mirror_rows.dtype)
    combined = keep + given + jnp.sum(returned.reshape(groups, 2, row_count, block_rows), axis=1)
    strip_rows = jnp.transpose(combined, (1, 0, 2)).reshape(row_count, groups * block_rows)
    return lax.psum_scatter(strip_rows, "par", scatter_dimension=1, tiled=True)


def solution(mesh):
    in_specs = (P("ex", "par"),)
    out_specs = P("ex", "par")
    return jax.shard_map(shards, mesh=mesh, in_specs=in_specs, out_specs=out_specs, check_vma=False)
```

profile of v0, /device:TPU:4, one launch (start us, length us, event | category | flops | bytes accessed | tf_op | source)
XLA Modules:
  0.0 449.9 jit_solution(4470708398375117228)
XLA Ops:
  6.5 1.4 constant_dynamic-slice_fusion.2
  7.9 7.8 %collective-permute-start = (bf16[80,4096]{1,0:T(8,128)(2,1)S(1)}, bf16[80,4096]{1,0:T(8,128)(2,1)S(1)}, u32[]{:S(2)}, u32[]{:S(2)}) collective-permute-start(bf16[80,4096]{1,0:T(8,128)(2,1)S(1)} %get-tuple-element.6), channel_id=1, source_target_pairs={{0,16},{16,0},{32,48},{48,32},{64,80},{80,64},{96,112},{112,96},{1... | collective-permute-start | bytes 1966088 | tf_op jit(solution)/shard_map/ppermute | solution.py:10
  15.7 12.1 %collective-permute-done = bf16[80,4096]{1,0:T(8,128)(2,1)S(1)} collective-permute-done((bf16[80,4096]{1,0:T(8,128)(2,1)S(1)}, bf16[80,4096]{1,0:T(8,128)(2,1)S(1)}, u32[]{:S(2)}, u32[]{:S(2)}) %collective-permute-start) | collective-permute-done | bytes 655392 | tf_op jit(solution)/shard_map/ppermute | solution.py:10
  28.1 11.4 %collective-permute-start.1 = (bf16[160,4096]{1,0:T(8,128)(2,1)S(1)}, bf16[160,4096]{1,0:T(8,128)(2,1)S(1)}, u32[]{:S(2)}, u32[]{:S(2)}) collective-permute-start(bf16[160,4096]{1,0:T(8,128)(2,1)S(1)} %maximum_select_fusion), channel_id=1, source_target_pairs={{32,0},{48,16},{64,32},{80,48},{96,64},{112,80},{128,96},{144,112}... | collective-permute-start | bytes 3932168 | tf_op jit(solution)/shard_map/ppermute | solution.py:16
  39.5 27.1 %collective-permute-done.1 = bf16[160,4096]{1,0:T(8,128)(2,1)S(1)} collective-permute-done((bf16[160,4096]{1,0:T(8,128)(2,1)S(1)}, bf16[160,4096]{1,0:T(8,128)(2,1)S(1)}, u32[]{:S(2)}, u32[]{:S(2)}) %collective-permute-start.1) | collective-permute-done | bytes 1310752 | tf_op jit(solution)/shard_map/ppermute | solution.py:16
  66.6 5.6 %collective-permute-start.2 = (bf16[160,4096]{1,0:T(8,128)(2,1)S(1)}, bf16[160,4096]{1,0:T(8,128)(2,1)S(1)}, u32[]{:S(2)}, u32[]{:S(2)}) collective-permute-start(bf16[160,4096]{1,0:T(8,128)(2,1)S(1)} %collective-permute-done.1), channel_id=1, source_target_pairs={{32,0},{48,16},{64,32},{80,48},{96,64},{112,80},{128,96},{144,112}... | collective-permute-start | bytes 3932168 | tf_op jit(solution)/shard_map/ppermute | solution.py:16
  72.2 26.2 %collective-permute-done.2 = bf16[160,4096]{1,0:T(8,128)(2,1)S(1)} collective-permute-done((bf16[160,4096]{1,0:T(8,128)(2,1)S(1)}, bf16[160,4096]{1,0:T(8,128)(2,1)S(1)}, u32[]{:S(2)}, u32[]{:S(2)}) %collective-permute-start.2) | collective-permute-done | bytes 1310752 | tf_op jit(solution)/shard_map/ppermute | solution.py:16
  98.4 5.6 %collective-permute-start.3 = (bf16[160,4096]{1,0:T(8,128)(2,1)S(1)}, bf16[160,4096]{1,0:T(8,128)(2,1)S(1)}, u32[]{:S(2)}, u32[]{:S(2)}) collective-permute-start(bf16[160,4096]{1,0:T(8,128)(2,1)S(1)} %collective-permute-done.2), channel_id=1, source_target_pairs={{32,0},{48,16},{64,32},{80,48},{96,64},{112,80},{128,96},{144,112}... | collective-permute-start | bytes 3932168 | tf_op jit(solution)/shard_map/ppermute | solution.py:16
  104.0 25.3 %collective-permute-done.3 = bf16[160,4096]{1,0:T(8,128)(2,1)S(1)} collective-permute-done((bf16[160,4096]{1,0:T(8,128)(2,1)S(1)}, bf16[160,4096]{1,0:T(8,128)(2,1)S(1)}, u32[]{:S(2)}, u32[]{:S(2)}) %collective-permute-start.3) | collective-permute-done | bytes 1310752 | tf_op jit(solution)/shard_map/ppermute | solution.py:16
  130.4 5.6 %collective-permute-start.4 = (bf16[160,4096]{1,0:T(8,128)(2,1)S(1)}, bf16[160,4096]{1,0:T(8,128)(2,1)S(1)}, u32[]{:S(2)}, u32[]{:S(2)}) collective-permute-start(bf16[160,4096]{1,0:T(8,128)(2,1)S(1)} %collective-permute-done.3), channel_id=1, source_target_pairs={{32,0},{48,16},{64,32},{80,48},{96,64},{112,80},{128,96},{144,112}... | collective-permute-start | bytes 3932168 | tf_op jit(solution)/shard_map/ppermute | solution.py:16
  136.0 24.4 %collective-permute-done.4 = bf16[160,4096]{1,0:T(8,128)(2,1)S(1)} collective-permute-done((bf16[160,4096]{1,0:T(8,128)(2,1)S(1)}, bf16[160,4096]{1,0:T(8,128)(2,1)S(1)}, u32[]{:S(2)}, u32[]{:S(2)}) %collective-permute-start.4) | collective-permute-done | bytes 1310752 | tf_op jit(solution)/shard_map/ppermute | solution.py:16
  161.5 5.6 %collective-permute-start.5 = (bf16[160,4096]{1,0:T(8,128)(2,1)S(1)}, bf16[160,4096]{1,0:T(8,128)(2,1)}, u32[]{:S(2)}, u32[]{:S(2)}) collective-permute-start(bf16[160,4096]{1,0:T(8,128)(2,1)S(1)} %collective-permute-done.4), channel_id=1, source_target_pairs={{32,0},{48,16},{64,32},{80,48},{96,64},{112,80},{128,96},{144,112}... | collective-permute-start | bytes 3932168 | tf_op jit(solution)/shard_map/ppermute | solution.py:16
  167.1 23.5 %collective-permute-done.5 = bf16[160,4096]{1,0:T(8,128)(2,1)} collective-permute-done((bf16[160,4096]{1,0:T(8,128)(2,1)S(1)}, bf16[160,4096]{1,0:T(8,128)(2,1)}, u32[]{:S(2)}, u32[]{:S(2)}) %collective-permute-start.5) | collective-permute-done | bytes 1310752 | tf_op jit(solution)/shard_map/ppermute | solution.py:16
  190.5 5.7 %collective-permute-start.6 = (bf16[160,4096]{1,0:T(8,128)(2,1)}, bf16[160,4096]{1,0:T(8,128)(2,1)}, u32[]{:S(2)}, u32[]{:S(2)}) collective-permute-start(bf16[160,4096]{1,0:T(8,128)(2,1)} %collective-permute-done.5), channel_id=1, source_target_pairs={{32,0},{48,16},{64,32},{80,48},{96,64},{112,80},{128,96},{144,112}... | collective-permute-start | bytes 3932168 | tf_op jit(solution)/shard_map/ppermute | solution.py:16
  196.5 7.4 %collective-permute-start.8 = (bf16[160,2048]{1,0:T(8,128)(2,1)S(1)}, bf16[160,2048]{1,0:T(8,128)(2,1)S(1)}, u32[]{:S(2)}, u32[]{:S(2)}) collective-permute-start(bf16[160,2048]{1,0:T(8,128)(2,1)S(1)} %constant_dynamic-slice_fusion), channel_id=1, source_target_pairs={{256,0},{272,16},{288,32},{304,48},{320,64},{336,80},{352,96},{368... | collective-permute-start | bytes 1966088 | tf_op jit(solution)/shard_map/ppermute | solution.py:16
  204.7 74.4 %collective-permute-done.6 = bf16[160,4096]{1,0:T(8,128)(2,1)} collective-permute-done((bf16[160,4096]{1,0:T(8,128)(2,1)}, bf16[160,4096]{1,0:T(8,128)(2,1)}, u32[]{:S(2)}, u32[]{:S(2)}) %collective-permute-start.6) | collective-permute-done | bytes 1310752 | tf_op jit(solution)/shard_map/ppermute | solution.py:16
  279.1 5.8 %collective-permute-start.7 = (bf16[160,4096]{1,0:T(8,128)(2,1)}, bf16[160,4096]{1,0:T(8,128)(2,1)S(1)}, u32[]{:S(2)}, u32[]{:S(2)}) collective-permute-start(bf16[160,4096]{1,0:T(8,128)(2,1)} %collective-permute-done.6), channel_id=1, source_target_pairs={{32,0},{48,16},{64,32},{80,48},{96,64},{112,80},{128,96},{144,112}... | collective-permute-start | bytes 3932168 | tf_op jit(solution)/shard_map/ppermute | solution.py:16
  284.9 1.2 bitcast_dynamic-update-slice_fusion.6
  286.2 1.2 bitcast_dynamic-update-slice_fusion.5
  288.0 1.8 bitcast_dynamic-update-slice_fusion.3
  289.9 1.8 bitcast_dynamic-update-slice_fusion.2
  291.7 11.6 %collective-permute-done.7 = bf16[160,4096]{1,0:T(8,128)(2,1)S(1)} collective-permute-done((bf16[160,4096]{1,0:T(8,128)(2,1)}, bf16[160,4096]{1,0:T(8,128)(2,1)S(1)}, u32[]{:S(2)}, u32[]{:S(2)}) %collective-permute-start.7) | collective-permute-done | bytes 1310752 | tf_op jit(solution)/shard_map/ppermute | solution.py:16
  304.9 1.2 convert_element_type.15
  306.2 11.0 %all-to-all-start = ((bf16[32,80,160]{2,1,0:T(8,128)(2,1)}), bf16[32,80,160]{2,1,0:T(8,128)(2,1)S(1)}, u32[]{:S(2)}, u32[]{:S(2)}) async-start(bf16[32,80,160]{2,1,0:T(8,128)(2,1)} %bitcast.72), calls=%async_computation | async-start | bytes 2621440 | tf_op jit(solution)/shard_map/all_to_all | solution.py:74
  318.0 1.5 copy-done
  326.7 2.2 dynamic-slice_convert_fusion
  329.0 2.1 collective-permute-start.9
  331.1 44.6 %all-to-all-done = bf16[32,80,160]{2,1,0:T(8,128)(2,1)S(1)} async-done(((bf16[32,80,160]{2,1,0:T(8,128)(2,1)}), bf16[32,80,160]{2,1,0:T(8,128)(2,1)S(1)}, u32[]{:S(2)}, u32[]{:S(2)}) %all-to-all-start) | async-done | bytes 819232 | tf_op jit(solution)/shard_map/all_to_all | solution.py:74
  376.0 1.5 copy-done.1
  377.7 1.6 copy.31
  379.3 62.1 %reduce-scatter.4.cloned.1.call-done = f32[160,80]{1,0:T(8,128)} async-done(((f32[2560,80]{1,0:T(8,128)}), f32[160,80]{1,0:T(8,128)}) %reduce-scatter.4.cloned.1.call-update) | async-done | bytes 51216
  441.5 1.6 copy.30
  (49 shorter events, 14.0 us)
Async XLA Ops:
  7.9 19.9 %collective-permute-start = (bf16[80,4096]{1,0:T(8,128)(2,1)S(1)}, bf16[80,4096]{1,0:T(8,128)(2,1)S(1)}, u32[]{:S(2)}, u32[]{:S(2)}) collective-permute-start(bf16[80,4096]{1,0:T(8,128)(2,1)S(1)} %get-tuple-element.6), channel_id=1, source_target_pairs={{0,16},{16,0},{32,48},{48,32},{64,80},{80,64},{96,112},{112,96},{1... | collective-permute-start | bytes 1966088 | tf_op jit(solution)/shard_map/ppermute | solution.py:10
  28.1 38.6 %collective-permute-start.1 = (bf16[160,4096]{1,0:T(8,128)(2,1)S(1)}, bf16[160,4096]{1,0:T(8,128)(2,1)S(1)}, u32[]{:S(2)}, u32[]{:S(2)}) collective-permute-start(bf16[160,4096]{1,0:T(8,128)(2,1)S(1)} %maximum_select_fusion), channel_id=1, source_target_pairs={{32,0},{48,16},{64,32},{80,48},{96,64},{112,80},{128,96},{144,112}... | collective-permute-start | bytes 3932168 | tf_op jit(solution)/shard_map/ppermute | solution.py:16
  66.6 5.6 %copy-start.6 = (bf16[160,4096]{1,0:T(8,128)(2,1)}, bf16[160,4096]{1,0:T(8,128)(2,1)S(1)}, u32[]{:S(2)}) copy-start(bf16[160,4096]{1,0:T(8,128)(2,1)S(1)} %collective-permute-done.1) | copy-start | bytes 3932164
  66.6 31.8 %collective-permute-start.2 = (bf16[160,4096]{1,0:T(8,128)(2,1)S(1)}, bf16[160,4096]{1,0:T(8,128)(2,1)S(1)}, u32[]{:S(2)}, u32[]{:S(2)}) collective-permute-start(bf16[160,4096]{1,0:T(8,128)(2,1)S(1)} %collective-permute-done.1), channel_id=1, source_target_pairs={{32,0},{48,16},{64,32},{80,48},{96,64},{112,80},{128,96},{144,112}... | collective-permute-start | bytes 3932168 | tf_op jit(solution)/shard_map/ppermute | solution.py:16
  98.4 30.9 %collective-permute-start.3 = (bf16[160,4096]{1,0:T(8,128)(2,1)S(1)}, bf16[160,4096]{1,0:T(8,128)(2,1)S(1)}, u32[]{:S(2)}, u32[]{:S(2)}) collective-permute-start(bf16[160,4096]{1,0:T(8,128)(2,1)S(1)} %collective-permute-done.2), channel_id=1, source_target_pairs={{32,0},{48,16},{64,32},{80,48},{96,64},{112,80},{128,96},{144,112}... | collective-permute-start | bytes 3932168 | tf_op jit(solution)/shard_map/ppermute | solution.py:16
  129.3 1.1 copy-start.2
  130.4 30.0 %collective-permute-start.4 = (bf16[160,4096]{1,0:T(8,128)(2,1)S(1)}, bf16[160,4096]{1,0:T(8,128)(2,1)S(1)}, u32[]{:S(2)}, u32[]{:S(2)}) collective-permute-start(bf16[160,4096]{1,0:T(8,128)(2,1)S(1)} %collective-permute-done.3), channel_id=1, source_target_pairs={{32,0},{48,16},{64,32},{80,48},{96,64},{112,80},{128,96},{144,112}... | collective-permute-start | bytes 3932168 | tf_op jit(solution)/shard_map/ppermute | solution.py:16
  160.4 1.1 copy-start.4
  161.5 29.1 %collective-permute-start.5 = (bf16[160,4096]{1,0:T(8,128)(2,1)S(1)}, bf16[160,4096]{1,0:T(8,128)(2,1)}, u32[]{:S(2)}, u32[]{:S(2)}) collective-permute-start(bf16[160,4096]{1,0:T(8,128)(2,1)S(1)} %collective-permute-done.4), channel_id=1, source_target_pairs={{32,0},{48,16},{64,32},{80,48},{96,64},{112,80},{128,96},{144,112}... | collective-permute-start | bytes 3932168 | tf_op jit(solution)/shard_map/ppermute | solution.py:16
  190.5 88.5 %collective-permute-start.6 = (bf16[160,4096]{1,0:T(8,128)(2,1)}, bf16[160,4096]{1,0:T(8,128)(2,1)}, u32[]{:S(2)}, u32[]{:S(2)}) collective-permute-start(bf16[160,4096]{1,0:T(8,128)(2,1)} %collective-permute-done.5), channel_id=1, source_target_pairs={{32,0},{48,16},{64,32},{80,48},{96,64},{112,80},{128,96},{144,112}... | collective-permute-start | bytes 3932168 | tf_op jit(solution)/shard_map/ppermute | solution.py:16
  196.5 7.6 %copy-start.7 = (bf16[160,4096]{1,0:T(8,128)(2,1)S(1)}, bf16[160,4096]{1,0:T(8,128)(2,1)}, u32[]{:S(2)}) copy-start(bf16[160,4096]{1,0:T(8,128)(2,1)} %copy-done.6) | copy-start | bytes 3932164
  196.5 107.4 %collective-permute-start.8 = (bf16[160,2048]{1,0:T(8,128)(2,1)S(1)}, bf16[160,2048]{1,0:T(8,128)(2,1)S(1)}, u32[]{:S(2)}, u32[]{:S(2)}) collective-permute-start(bf16[160,2048]{1,0:T(8,128)(2,1)S(1)} %constant_dynamic-slice_fusion), channel_id=1, source_target_pairs={{256,0},{272,16},{288,32},{304,48},{320,64},{336,80},{352,96},{368... | collective-permute-start | bytes 1966088 | tf_op jit(solution)/shard_map/ppermute | solution.py:16
  279.1 24.3 %collective-permute-start.7 = (bf16[160,4096]{1,0:T(8,128)(2,1)}, bf16[160,4096]{1,0:T(8,128)(2,1)S(1)}, u32[]{:S(2)}, u32[]{:S(2)}) collective-permute-start(bf16[160,4096]{1,0:T(8,128)(2,1)} %collective-permute-done.6), channel_id=1, source_target_pairs={{32,0},{48,16},{64,32},{80,48},{96,64},{112,80},{128,96},{144,112}... | collective-permute-start | bytes 3932168 | tf_op jit(solution)/shard_map/ppermute | solution.py:16
  284.9 1.3 copy-start.3
  286.2 1.3 copy-start.5
  306.2 69.6 %all-to-all-start = ((bf16[32,80,160]{2,1,0:T(8,128)(2,1)}), bf16[32,80,160]{2,1,0:T(8,128)(2,1)S(1)}, u32[]{:S(2)}, u32[]{:S(2)}) async-start(bf16[32,80,160]{2,1,0:T(8,128)(2,1)} %bitcast.72), calls=%async_computation | async-start | bytes 2621440 | tf_op jit(solution)/shard_map/all_to_all | solution.py:74
  317.1 124.3 %reduce-scatter.4.cloned.1.call-start = ((), (), s32[]{:S(2)}) async-start(), calls=%async_computation.2 | async-start | bytes 1392640
  318.0 1.5 copy-start
  319.5 2.5 copy-start.8
  322.1 3.2 copy-start.9
  329.0 47.0 %collective-permute-start.9 = (bf16[16,80,160]{2,1,0:T(8,128)(2,1)}, bf16[16,80,160]{2,1,0:T(8,128)(2,1)S(1)}, u32[]{:S(2)}, u32[]{:S(2)}) collective-permute-start(bf16[16,80,160]{2,1,0:T(8,128)(2,1)} %dynamic-slice_convert_fusion), channel_id=1, source_target_pairs={{0,16},{16,0},{32,48},{48,32},{64,80},{80,64},{96,112},{112,96},{1... | collective-permute-start | bytes 1228808 | tf_op jit(solution)/shard_map/ppermute | solution.py:10
  375.7 1.7 copy-start.1
Sparse Core Ops, SparseCore 0:
  379.4 61.9 reduce-scatter.3
where the time goes:
time: 451 us; the launch traced here: 450 us
  waiting for transfers between devices  331 us (73%)
  starting transfers between devices  73.6 us (16%)
  local copies, waits for them, and re-layouts  20 us (4%)
  between operations  14 us (3%)
  matrix products  9.11 us (2%)
    ppermute x8, waiting for transfers between devices, from_behind(): return lax.ppermute(block, axis, route)  212 us
    unnamed x2, waiting for transfers between devices  62.1 us
    ppermute x8, starting transfers between devices, from_behind(): return lax.ppermute(block, axis, route)  52.6 us
    all_to_all x1, waiting for transfers between devices, shards(): lax.all_to_all(mirror_rows.astype(jnp.bfloat16), 'ex', split_axis=0, conc...  44.6 us
    ppermute x2, waiting for transfers between devices, partner_2(): return lax.ppermute(value, axis, pairs)  12.1 us
    all_to_all x1, starting transfers between devices, shards(): lax.all_to_all(mirror_rows.astype(jnp.bfloat16), 'ex', split_axis=0, conc...  11 us
    ppermute x2, starting transfers between devices, partner_2(): return lax.ppermute(value, axis, pairs)  9.93 us
    dot_general x9, matrix products, tile_of(): lax.dot_general(rows_a, rows_b, (((1,), (1,)), ((), ())), preferred_eleme...  9.11 us
  transfers between devices with their start and end apart: 12, of which 10 were waited for; matrix products, arithmetic and copies ran while one was open for 4% of the time, Pallas kernels for 0%

commit v1 on v0

v1 whole, which is shorter than its diff:
```python
import jax
import jax.numpy as jnp
from jax import lax
from jax.sharding import PartitionSpec as P

CHUNKS = 2
AXES = ("ex", "par")


def tile_of(rows_a, rows_b):
    return lax.dot_general(
        rows_a, rows_b, (((1,), (1,)), ((), ())), preferred_element_type=jnp.float32
    )


def shards(jacobian):
    ex_size, par_size = lax.axis_size("ex"), lax.axis_size("par")
    planes = ex_size // 2
    half = planes // 2
    position, column = lax.axis_index("ex"), lax.axis_index("par")
    plane, member, core = position // 2, position % 2, column % 2
    way = 1 - 2 * core
    rows, cols = jacobian.shape
    pair_cols = cols // 2
    width = pair_cols // CHUNKS
    swap = [(i, i ^ 1) for i in range(ex_size)]
    onward = [
        (i * par_size + p, ((i + (2 if p % 2 == 0 else -2)) % ex_size) * par_size + p)
        for i in range(ex_size)
        for p in range(par_size)
    ]

    def pair_block(index):
        out = lax.dynamic_slice_in_dim(jacobian, (1 - member) * pair_cols + index * width, width, 1)
        got = lax.ppermute(out, "ex", swap)
        mine = lax.dynamic_slice_in_dim(jacobian, member * pair_cols + index * width, width, 1)
        return jnp.where(
            member == 0, jnp.concatenate([mine, got], 0), jnp.concatenate([got, mine], 0)
        )

    own = [pair_block(c) for c in range(CHUNKS)]
    strip = jnp.zeros((2, planes, rows, 2 * rows), jnp.bfloat16)

    def put(strip, tile, where):
        block = tile.astype(jnp.bfloat16).reshape(2, 1, rows, 2 * rows)
        return lax.dynamic_update_slice_in_dim(strip, block, jnp.mod(where, planes), 1)

    strip = put(strip, sum(tile_of(own[c], own[c]) for c in range(CHUNKS)), plane)
    travel = list(own)
    for step in range(1, half):
        for c in range(CHUNKS):
            travel[c] = lax.ppermute(travel[c], AXES, onward)
        tile = sum(tile_of(own[c], travel[c]) for c in range(CHUNKS))
        strip = put(strip, tile, plane - way * step)
    theirs = jnp.mod(plane + way, planes) // half
    got = lax.ppermute(jnp.where(theirs == 0, travel[0], travel[1]), AXES, onward)
    strip = put(strip, tile_of(jnp.where(plane // half == 0, own[0], own[1]), got), plane + half)

    groups = [
        [(2 * z + m) * par_size + p for m in range(2) for p in range(par_size)]
        for z in range(planes)
    ]
    parts = strip.reshape(2 * planes, rows, 2 * rows)
    parts = lax.all_to_all(parts, AXES, 0, 0, axis_index_groups=groups, tiled=True)
    mine = jnp.sum(parts.astype(jnp.float32), axis=0)

    def mirror(across):
        pairs = [
            ((2 * z + m) * par_size + p, (2 * p + (m ^ across)) * par_size + z)
            for z in range(planes)
            for m in range(2)
            for p in range(par_size)
            if p != z
        ]
        block = lax.dynamic_slice_in_dim(mine, (member ^ across) * rows, rows, 1)
        return lax.ppermute(block.T, AXES, pairs)

    same, other = mirror(0), mirror(1)
    added = jnp.where(
        member == 0, jnp.concatenate([same, other], 1), jnp.concatenate([other, same], 1)
    )
    return mine + added


def solution(mesh):
    return jax.shard_map(
        shards, mesh=mesh, in_specs=(P("ex", "par"),), out_specs=P("ex", "par"), check_vma=False
    )
```

time: 451 us -> 197 us (0.44)
  the two profiles are of different devices: /device:TPU:4 before, /device:TPU:16 now
where the time goes in v1:
time: 197 us
  waiting for transfers between devices  115 us (58%)
  starting transfers between devices  64.6 us (33%)
  local copies, waits for them, and re-layouts  8.59 us (4%)
  matrix products  6.94 us (4%)
    ppermute x14, waiting for transfers between devices, shards(): travel[c] = lax.ppermute(travel[c], AXES, onward)  67.2 us
    ppermute x14, starting transfers between devices, shards(): travel[c] = lax.ppermute(travel[c], AXES, onward)  30.6 us
    all_to_all x1, waiting for transfers between devices, shards(): lax.all_to_all(parts, AXES, 0, 0, axis_index_groups=groups, tiled=True)  18.4 us
    ppermute x2, starting transfers between devices, mirror(): return lax.ppermute(block.T, AXES, pairs)  17.4 us
    ppermute x2, waiting for transfers between devices, mirror(): return lax.ppermute(block.T, AXES, pairs)  10.7 us
    ppermute x1, waiting for transfers between devices, shards(): lax.ppermute(jnp.where(theirs == 0, travel[0], travel[1]), AXES, onward)  9.76 us
    ppermute x2, waiting for transfers between devices, pair_block(): got = lax.ppermute(out, 'ex', swap)  8.53 us
    all_to_all x1, starting transfers between devices, shards(): lax.all_to_all(parts, AXES, 0, 0, axis_index_groups=groups, tiled=True)  7.43 us
  transfers between devices with their start and end apart: 20, of which 20 were waited for; matrix products, arithmetic and copies ran while one was open for 7% of the time, Pallas kernels for 0%

profile of v1, /device:TPU:16, one launch (start us, length us, event | category | flops | bytes accessed | tf_op | source)
XLA Modules:
  0.0 196.7 jit_solution(8529752714132175387)
XLA Ops:
  1.4 4.9 %collective-permute-start.1 = (bf16[80,2048]{1,0:T(8,128)(2,1)S(1)}, bf16[80,2048]{1,0:T(8,128)(2,1)S(1)}, u32[]{:S(2)}, u32[]{:S(2)}) collective-permute-start(bf16[80,2048]{1,0:T(8,128)(2,1)S(1)} %get-tuple-element.7), channel_id=1, source_target_pairs={{0,16},{16,0},{32,48},{48,32},{64,80},{80,64},{96,112},{112,96},{1... | collective-permute-start | bytes 983048 | tf_op jit(solution)/shard_map/ppermute | solution.py:35
  6.3 2.4 %collective-permute-start = (bf16[80,2048]{1,0:T(8,128)(2,1)S(1)}, bf16[80,2048]{1,0:T(8,128)(2,1)S(1)}, u32[]{:S(2)}, u32[]{:S(2)}) collective-permute-start(bf16[80,2048]{1,0:T(8,128)(2,1)S(1)} %get-tuple-element.6), channel_id=1, source_target_pairs={{0,16},{16,0},{32,48},{48,32},{64,80},{80,64},{96,112},{112,96},{1... | collective-permute-start | bytes 983048 | tf_op jit(solution)/shard_map/ppermute | solution.py:35
  8.7 6.6 %collective-permute-done.1 = bf16[80,2048]{1,0:T(8,128)(2,1)S(1)} collective-permute-done((bf16[80,2048]{1,0:T(8,128)(2,1)S(1)}, bf16[80,2048]{1,0:T(8,128)(2,1)S(1)}, u32[]{:S(2)}, u32[]{:S(2)}) %collective-permute-start.1) | collective-permute-done | bytes 327712 | tf_op jit(solution)/shard_map/ppermute | solution.py:35
  15.5 3.8 %collective-permute-start.3 = (bf16[160,2048]{1,0:T(8,128)(2,1)S(1)}, bf16[160,2048]{1,0:T(8,128)(2,1)S(1)}, u32[]{:S(2)}, u32[]{:S(2)}) collective-permute-start(bf16[160,2048]{1,0:T(8,128)(2,1)S(1)} %maximum_select_fusion.1), channel_id=1, source_target_pairs={{0,32},{1,481},{2,34},{3,483},{4,36},{5,485},{6,38},{7,487},{8,40}... | collective-permute-start | bytes 1966088 | tf_op jit(solution)/shard_map/ppermute | solution.py:52
  21.4 3.8 %collective-permute-start.2 = (bf16[160,2048]{1,0:T(8,128)(2,1)S(1)}, bf16[160,2048]{1,0:T(8,128)(2,1)S(1)}, u32[]{:S(2)}, u32[]{:S(2)}) collective-permute-start(bf16[160,2048]{1,0:T(8,128)(2,1)S(1)} %maximum_select_fusion), channel_id=1, source_target_pairs={{0,32},{1,481},{2,34},{3,483},{4,36},{5,485},{6,38},{7,487},{8,40}... | collective-permute-start | bytes 1966088 | tf_op jit(solution)/shard_map/ppermute | solution.py:52
  25.2 10.3 %collective-permute-done.3 = bf16[160,2048]{1,0:T(8,128)(2,1)S(1)} collective-permute-done((bf16[160,2048]{1,0:T(8,128)(2,1)S(1)}, bf16[160,2048]{1,0:T(8,128)(2,1)S(1)}, u32[]{:S(2)}, u32[]{:S(2)}) %collective-permute-start.3) | collective-permute-done | bytes 655392 | tf_op jit(solution)/shard_map/ppermute | solution.py:52
  37.4 5.1 %collective-permute-done.2 = bf16[160,2048]{1,0:T(8,128)(2,1)S(1)} collective-permute-done((bf16[160,2048]{1,0:T(8,128)(2,1)S(1)}, bf16[160,2048]{1,0:T(8,128)(2,1)S(1)}, u32[]{:S(2)}, u32[]{:S(2)}) %collective-permute-start.2) | collective-permute-done | bytes 655392 | tf_op jit(solution)/shard_map/ppermute | solution.py:52
  42.5 1.9 collective-permute-start.4
  44.7 4.8 %collective-permute-done.5 = bf16[160,2048]{1,0:T(8,128)(2,1)S(1)} collective-permute-done((bf16[160,2048]{1,0:T(8,128)(2,1)S(1)}, bf16[160,2048]{1,0:T(8,128)(2,1)S(1)}, u32[]{:S(2)}, u32[]{:S(2)}) %collective-permute-start.5) | collective-permute-done | bytes 655392 | tf_op jit(solution)/shard_map/ppermute | solution.py:52
  51.4 5.2 %collective-permute-done.4 = bf16[160,2048]{1,0:T(8,128)(2,1)} collective-permute-done((bf16[160,2048]{1,0:T(8,128)(2,1)S(1)}, bf16[160,2048]{1,0:T(8,128)(2,1)}, u32[]{:S(2)}, u32[]{:S(2)}) %collective-permute-start.4) | collective-permute-done | bytes 655392 | tf_op jit(solution)/shard_map/ppermute | solution.py:52
  61.4 2.1 %collective-permute-done.7 = bf16[160,2048]{1,0:T(8,128)(2,1)S(1)} collective-permute-done((bf16[160,2048]{1,0:T(8,128)(2,1)S(1)}, bf16[160,2048]{1,0:T(8,128)(2,1)S(1)}, u32[]{:S(2)}, u32[]{:S(2)}) %collective-permute-start.7) | collective-permute-done | bytes 655392 | tf_op jit(solution)/shard_map/ppermute | solution.py:52
  63.5 1.9 collective-permute-start.9
  65.5 5.1 %collective-permute-done.6 = bf16[160,2048]{1,0:T(8,128)(2,1)S(1)} collective-permute-done((bf16[160,2048]{1,0:T(8,128)(2,1)}, bf16[160,2048]{1,0:T(8,128)(2,1)S(1)}, u32[]{:S(2)}, u32[]{:S(2)}) %collective-permute-start.6) | collective-permute-done | bytes 655392 | tf_op jit(solution)/shard_map/ppermute | solution.py:52
  70.6 1.9 collective-permute-start.8
  75.3 2.3 %collective-permute-done.9 = bf16[160,2048]{1,0:T(8,128)(2,1)S(1)} collective-permute-done((bf16[160,2048]{1,0:T(8,128)(2,1)S(1)}, bf16[160,2048]{1,0:T(8,128)(2,1)S(1)}, u32[]{:S(2)}, u32[]{:S(2)}) %collective-permute-start.9) | collective-permute-done | bytes 655392 | tf_op jit(solution)/shard_map/ppermute | solution.py:52
  79.5 5.1 %collective-permute-done.8 = bf16[160,2048]{1,0:T(8,128)(2,1)S(1)} collective-permute-done((bf16[160,2048]{1,0:T(8,128)(2,1)S(1)}, bf16[160,2048]{1,0:T(8,128)(2,1)S(1)}, u32[]{:S(2)}, u32[]{:S(2)}) %collective-permute-start.8) | collective-permute-done | bytes 655392 | tf_op jit(solution)/shard_map/ppermute | solution.py:52
  88.5 3.1 %collective-permute-done.11 = bf16[160,2048]{1,0:T(8,128)(2,1)S(1)} collective-permute-done((bf16[160,2048]{1,0:T(8,128)(2,1)S(1)}, bf16[160,2048]{1,0:T(8,128)(2,1)S(1)}, u32[]{:S(2)}, u32[]{:S(2)}) %collective-permute-start.11) | collective-permute-done | bytes 655392 | tf_op jit(solution)/shard_map/ppermute | solution.py:52
  91.6 1.9 collective-permute-start.13
  93.5 5.1 %collective-permute-done.10 = bf16[160,2048]{1,0:T(8,128)(2,1)S(1)} collective-permute-done((bf16[160,2048]{1,0:T(8,128)(2,1)S(1)}, bf16[160,2048]{1,0:T(8,128)(2,1)S(1)}, u32[]{:S(2)}, u32[]{:S(2)}) %collective-permute-start.10) | collective-permute-done | bytes 655392 | tf_op jit(solution)/shard_map/ppermute | solution.py:52
  98.7 1.9 collective-permute-start.12
  102.3 3.4 %collective-permute-done.13 = bf16[160,2048]{1,0:T(8,128)(2,1)S(1)} collective-permute-done((bf16[160,2048]{1,0:T(8,128)(2,1)S(1)}, bf16[160,2048]{1,0:T(8,128)(2,1)S(1)}, u32[]{:S(2)}, u32[]{:S(2)}) %collective-permute-start.13) | collective-permute-done | bytes 655392 | tf_op jit(solution)/shard_map/ppermute | solution.py:52
  107.6 5.1 %collective-permute-done.12 = bf16[160,2048]{1,0:T(8,128)(2,1)S(1)} collective-permute-done((bf16[160,2048]{1,0:T(8,128)(2,1)S(1)}, bf16[160,2048]{1,0:T(8,128)(2,1)S(1)}, u32[]{:S(2)}, u32[]{:S(2)}) %collective-permute-start.12) | collective-permute-done | bytes 655392 | tf_op jit(solution)/shard_map/ppermute | solution.py:52
  116.3 3.4 %collective-permute-done.15 = bf16[160,2048]{1,0:T(8,128)(2,1)S(1)} collective-permute-done((bf16[160,2048]{1,0:T(8,128)(2,1)S(1)}, bf16[160,2048]{1,0:T(8,128)(2,1)S(1)}, u32[]{:S(2)}, u32[]{:S(2)}) %collective-permute-start.15) | collective-permute-done | bytes 655392 | tf_op jit(solution)/shard_map/ppermute | solution.py:52
  119.7 7.0 %collective-permute-done.14 = bf16[160,2048]{1,0:T(8,128)(2,1)S(1)} collective-permute-done((bf16[160,2048]{1,0:T(8,128)(2,1)S(1)}, bf16[160,2048]{1,0:T(8,128)(2,1)S(1)}, u32[]{:S(2)}, u32[]{:S(2)}) %collective-permute-start.14) | collective-permute-done | bytes 655392 | tf_op jit(solution)/shard_map/ppermute | solution.py:52
  126.8 1.9 collective-permute-start.16
  130.7 9.8 %collective-permute-done.16 = bf16[160,2048]{1,0:T(8,128)(2,1)S(1)} collective-permute-done((bf16[160,2048]{1,0:T(8,128)(2,1)S(1)}, bf16[160,2048]{1,0:T(8,128)(2,1)S(1)}, u32[]{:S(2)}, u32[]{:S(2)}) %collective-permute-start.16) | collective-permute-done | bytes 655392 | tf_op jit(solution)/shard_map/ppermute | solution.py:56
  141.5 7.4 %all-to-all-start = ((bf16[32,80,160]{2,1,0:T(8,128)(2,1)}), bf16[32,80,160]{2,1,0:T(8,128)(2,1)S(1)}, u32[]{:S(2)}, u32[]{:S(2)}) async-start(bf16[32,80,160]{2,1,0:T(8,128)(2,1)} %bitcast.18), calls=%async_computation | async-start | bytes 2621440 | tf_op jit(solution)/shard_map/all_to_all | solution.py:64
  149.0 18.4 %all-to-all-done = bf16[32,80,160]{2,1,0:T(8,128)(2,1)S(1)} async-done(((bf16[32,80,160]{2,1,0:T(8,128)(2,1)}), bf16[32,80,160]{2,1,0:T(8,128)(2,1)S(1)}, u32[]{:S(2)}, u32[]{:S(2)}) %all-to-all-start) | async-done | bytes 819232 | tf_op jit(solution)/shard_map/all_to_all | solution.py:64
  167.8 11.1 %collective-permute-start.18 = (f32[80,80]{1,0:T(8,128)S(1)}, f32[80,80]{1,0:T(8,128)S(1)}, u32[]{:S(2)}, u32[]{:S(2)}) collective-permute-start(f32[80,80]{1,0:T(8,128)S(1)} %bitcast.73), channel_id=1, source_target_pairs={{1,48},{2,80},{3,112},{4,144},{5,176},{6,208},{7,240},{8,272},{9,3... | collective-permute-start | bytes 76808 | tf_op jit(solution)/shard_map/ppermute | solution.py:76
  178.9 6.3 %collective-permute-start.17 = (f32[80,80]{1,0:T(8,128)S(1)}, f32[80,80]{1,0:T(8,128)S(1)}, u32[]{:S(2)}, u32[]{:S(2)}) collective-permute-start(f32[80,80]{1,0:T(8,128)S(1)} %bitcast.72), channel_id=1, source_target_pairs={{1,32},{2,64},{3,96},{4,128},{5,160},{6,192},{7,224},{8,256},{9,28... | collective-permute-start | bytes 76808 | tf_op jit(solution)/shard_map/ppermute | solution.py:76
  185.2 2.4 %collective-permute-done.18 = f32[80,80]{1,0:T(8,128)S(1)} collective-permute-done((f32[80,80]{1,0:T(8,128)S(1)}, f32[80,80]{1,0:T(8,128)S(1)}, u32[]{:S(2)}, u32[]{:S(2)}) %collective-permute-start.18) | collective-permute-done | bytes 25632 | tf_op jit(solution)/shard_map/ppermute | solution.py:76
  187.6 8.4 %collective-permute-done.17 = f32[80,80]{1,0:T(8,128)S(1)} collective-permute-done((f32[80,80]{1,0:T(8,128)S(1)}, f32[80,80]{1,0:T(8,128)S(1)}, u32[]{:S(2)}, u32[]{:S(2)}) %collective-permute-start.17) | collective-permute-done | bytes 25632 | tf_op jit(solution)/shard_map/ppermute | solution.py:76
  (44 shorter events, 32.1 us)
Async XLA Ops:
  1.4 14.0 %collective-permute-start.1 = (bf16[80,2048]{1,0:T(8,128)(2,1)S(1)}, bf16[80,2048]{1,0:T(8,128)(2,1)S(1)}, u32[]{:S(2)}, u32[]{:S(2)}) collective-permute-start(bf16[80,2048]{1,0:T(8,128)(2,1)S(1)} %get-tuple-element.7), channel_id=1, source_target_pairs={{0,16},{16,0},{32,48},{48,32},{64,80},{80,64},{96,112},{112,96},{1... | collective-permute-start | bytes 983048 | tf_op jit(solution)/shard_map/ppermute | solution.py:35
  6.3 14.9 %collective-permute-start = (bf16[80,2048]{1,0:T(8,128)(2,1)S(1)}, bf16[80,2048]{1,0:T(8,128)(2,1)S(1)}, u32[]{:S(2)}, u32[]{:S(2)}) collective-permute-start(bf16[80,2048]{1,0:T(8,128)(2,1)S(1)} %get-tuple-element.6), channel_id=1, source_target_pairs={{0,16},{16,0},{32,48},{48,32},{64,80},{80,64},{96,112},{112,96},{1... | collective-permute-start | bytes 983048 | tf_op jit(solution)/shard_map/ppermute | solution.py:35
  15.5 20.0 %collective-permute-start.3 = (bf16[160,2048]{1,0:T(8,128)(2,1)S(1)}, bf16[160,2048]{1,0:T(8,128)(2,1)S(1)}, u32[]{:S(2)}, u32[]{:S(2)}) collective-permute-start(bf16[160,2048]{1,0:T(8,128)(2,1)S(1)} %maximum_select_fusion.1), channel_id=1, source_target_pairs={{0,32},{1,481},{2,34},{3,483},{4,36},{5,485},{6,38},{7,487},{8,40}... | collective-permute-start | bytes 1966088 | tf_op jit(solution)/shard_map/ppermute | solution.py:52
  21.4 21.1 %collective-permute-start.2 = (bf16[160,2048]{1,0:T(8,128)(2,1)S(1)}, bf16[160,2048]{1,0:T(8,128)(2,1)S(1)}, u32[]{:S(2)}, u32[]{:S(2)}) collective-permute-start(bf16[160,2048]{1,0:T(8,128)(2,1)S(1)} %maximum_select_fusion), channel_id=1, source_target_pairs={{0,32},{1,481},{2,34},{3,483},{4,36},{5,485},{6,38},{7,487},{8,40}... | collective-permute-start | bytes 1966088 | tf_op jit(solution)/shard_map/ppermute | solution.py:52
  35.5 14.0 %collective-permute-start.5 = (bf16[160,2048]{1,0:T(8,128)(2,1)S(1)}, bf16[160,2048]{1,0:T(8,128)(2,1)S(1)}, u32[]{:S(2)}, u32[]{:S(2)}) collective-permute-start(bf16[160,2048]{1,0:T(8,128)(2,1)S(1)} %collective-permute-done.3), channel_id=1, source_target_pairs={{0,32},{1,481},{2,34},{3,483},{4,36},{5,485},{6,38},{7,487},{8,40}... | collective-permute-start | bytes 1966088 | tf_op jit(solution)/shard_map/ppermute | solution.py:52
  42.5 14.1 %collective-permute-start.4 = (bf16[160,2048]{1,0:T(8,128)(2,1)S(1)}, bf16[160,2048]{1,0:T(8,128)(2,1)}, u32[]{:S(2)}, u32[]{:S(2)}) collective-permute-start(bf16[160,2048]{1,0:T(8,128)(2,1)S(1)} %collective-permute-done.2), channel_id=1, source_target_pairs={{0,32},{1,481},{2,34},{3,483},{4,36},{5,485},{6,38},{7,487},{8,40}... | collective-permute-start | bytes 1966088 | tf_op jit(solution)/shard_map/ppermute | solution.py:52
  49.5 14.0 %collective-permute-start.7 = (bf16[160,2048]{1,0:T(8,128)(2,1)S(1)}, bf16[160,2048]{1,0:T(8,128)(2,1)S(1)}, u32[]{:S(2)}, u32[]{:S(2)}) collective-permute-start(bf16[160,2048]{1,0:T(8,128)(2,1)S(1)} %collective-permute-done.5), channel_id=1, source_target_pairs={{0,32},{1,481},{2,34},{3,483},{4,36},{5,485},{6,38},{7,487},{8,40}... | collective-permute-start | bytes 1966088 | tf_op jit(solution)/shard_map/ppermute | solution.py:52
  56.6 13.9 %collective-permute-start.6 = (bf16[160,2048]{1,0:T(8,128)(2,1)}, bf16[160,2048]{1,0:T(8,128)(2,1)S(1)}, u32[]{:S(2)}, u32[]{:S(2)}) collective-permute-start(bf16[160,2048]{1,0:T(8,128)(2,1)} %collective-permute-done.4), channel_id=1, source_target_pairs={{0,32},{1,481},{2,34},{3,483},{4,36},{5,485},{6,38},{7,487},{8,40}... | collective-permute-start | bytes 1966088 | tf_op jit(solution)/shard_map/ppermute | solution.py:52
  63.5 14.0 %collective-permute-start.9 = (bf16[160,2048]{1,0:T(8,128)(2,1)S(1)}, bf16[160,2048]{1,0:T(8,128)(2,1)S(1)}, u32[]{:S(2)}, u32[]{:S(2)}) collective-permute-start(bf16[160,2048]{1,0:T(8,128)(2,1)S(1)} %collective-permute-done.7), channel_id=1, source_target_pairs={{0,32},{1,481},{2,34},{3,483},{4,36},{5,485},{6,38},{7,487},{8,40}... | collective-permute-start | bytes 1966088 | tf_op jit(solution)/shard_map/ppermute | solution.py:52
  70.6 14.0 %collective-permute-start.8 = (bf16[160,2048]{1,0:T(8,128)(2,1)S(1)}, bf16[160,2048]{1,0:T(8,128)(2,1)S(1)}, u32[]{:S(2)}, u32[]{:S(2)}) collective-permute-start(bf16[160,2048]{1,0:T(8,128)(2,1)S(1)} %collective-permute-done.6), channel_id=1, source_target_pairs={{0,32},{1,481},{2,34},{3,483},{4,36},{5,485},{6,38},{7,487},{8,40}... | collective-permute-start | bytes 1966088 | tf_op jit(solution)/shard_map/ppermute | solution.py:52
  77.6 14.0 %collective-permute-start.11 = (bf16[160,2048]{1,0:T(8,128)(2,1)S(1)}, bf16[160,2048]{1,0:T(8,128)(2,1)S(1)}, u32[]{:S(2)}, u32[]{:S(2)}) collective-permute-start(bf16[160,2048]{1,0:T(8,128)(2,1)S(1)} %collective-permute-done.9), channel_id=1, source_target_pairs={{0,32},{1,481},{2,34},{3,483},{4,36},{5,485},{6,38},{7,487},{8,40}... | collective-permute-start | bytes 1966088 | tf_op jit(solution)/shard_map/ppermute | solution.py:52
  84.6 14.0 %collective-permute-start.10 = (bf16[160,2048]{1,0:T(8,128)(2,1)S(1)}, bf16[160,2048]{1,0:T(8,128)(2,1)S(1)}, u32[]{:S(2)}, u32[]{:S(2)}) collective-permute-start(bf16[160,2048]{1,0:T(8,128)(2,1)S(1)} %collective-permute-done.8), channel_id=1, source_target_pairs={{0,32},{1,481},{2,34},{3,483},{4,36},{5,485},{6,38},{7,487},{8,40}... | collective-permute-start | bytes 1966088 | tf_op jit(solution)/shard_map/ppermute | solution.py:52
  91.6 14.0 %collective-permute-start.13 = (bf16[160,2048]{1,0:T(8,128)(2,1)S(1)}, bf16[160,2048]{1,0:T(8,128)(2,1)S(1)}, u32[]{:S(2)}, u32[]{:S(2)}) collective-permute-start(bf16[160,2048]{1,0:T(8,128)(2,1)S(1)} %collective-permute-done.11), channel_id=1, source_target_pairs={{0,32},{1,481},{2,34},{3,483},{4,36},{5,485},{6,38},{7,487},{8,40}... | collective-permute-start | bytes 1966088 | tf_op jit(solution)/shard_map/ppermute | solution.py:52
  98.7 14.0 %collective-permute-start.12 = (bf16[160,2048]{1,0:T(8,128)(2,1)S(1)}, bf16[160,2048]{1,0:T(8,128)(2,1)S(1)}, u32[]{:S(2)}, u32[]{:S(2)}) collective-permute-start(bf16[160,2048]{1,0:T(8,128)(2,1)S(1)} %collective-permute-done.10), channel_id=1, source_target_pairs={{0,32},{1,481},{2,34},{3,483},{4,36},{5,485},{6,38},{7,487},{8,40}... | collective-permute-start | bytes 1966088 | tf_op jit(solution)/shard_map/ppermute | solution.py:52
  105.7 14.0 %collective-permute-start.15 = (bf16[160,2048]{1,0:T(8,128)(2,1)S(1)}, bf16[160,2048]{1,0:T(8,128)(2,1)S(1)}, u32[]{:S(2)}, u32[]{:S(2)}) collective-permute-start(bf16[160,2048]{1,0:T(8,128)(2,1)S(1)} %collective-permute-done.13), channel_id=1, source_target_pairs={{0,32},{1,481},{2,34},{3,483},{4,36},{5,485},{6,38},{7,487},{8,40}... | collective-permute-start | bytes 1966088 | tf_op jit(solution)/shard_map/ppermute | solution.py:52
  112.7 14.0 %collective-permute-start.14 = (bf16[160,2048]{1,0:T(8,128)(2,1)S(1)}, bf16[160,2048]{1,0:T(8,128)(2,1)S(1)}, u32[]{:S(2)}, u32[]{:S(2)}) collective-permute-start(bf16[160,2048]{1,0:T(8,128)(2,1)S(1)} %collective-permute-done.12), channel_id=1, source_target_pairs={{0,32},{1,481},{2,34},{3,483},{4,36},{5,485},{6,38},{7,487},{8,40}... | collective-permute-start | bytes 1966088 | tf_op jit(solution)/shard_map/ppermute | solution.py:52
  126.8 13.7 %collective-permute-start.16 = (bf16[160,2048]{1,0:T(8,128)(2,1)S(1)}, bf16[160,2048]{1,0:T(8,128)(2,1)S(1)}, u32[]{:S(2)}, u32[]{:S(2)}) collective-permute-start(bf16[160,2048]{1,0:T(8,128)(2,1)S(1)} %broadcast_select_fusion), channel_id=1, source_target_pairs={{0,32},{1,481},{2,34},{3,483},{4,36},{5,485},{6,38},{7,487},{8,40}... | collective-permute-start | bytes 1966088 | tf_op jit(solution)/shard_map/ppermute | solution.py:56
  141.5 25.8 %all-to-all-start = ((bf16[32,80,160]{2,1,0:T(8,128)(2,1)}), bf16[32,80,160]{2,1,0:T(8,128)(2,1)S(1)}, u32[]{:S(2)}, u32[]{:S(2)}) async-start(bf16[32,80,160]{2,1,0:T(8,128)(2,1)} %bitcast.18), calls=%async_computation | async-start | bytes 2621440 | tf_op jit(solution)/shard_map/all_to_all | solution.py:64
  167.8 19.8 %collective-permute-start.18 = (f32[80,80]{1,0:T(8,128)S(1)}, f32[80,80]{1,0:T(8,128)S(1)}, u32[]{:S(2)}, u32[]{:S(2)}) collective-permute-start(f32[80,80]{1,0:T(8,128)S(1)} %bitcast.73), channel_id=1, source_target_pairs={{1,48},{2,80},{3,112},{4,144},{5,176},{6,208},{7,240},{8,272},{9,3... | collective-permute-start | bytes 76808 | tf_op jit(solution)/shard_map/ppermute | solution.py:76
  178.9 17.0 %collective-permute-start.17 = (f32[80,80]{1,0:T(8,128)S(1)}, f32[80,80]{1,0:T(8,128)S(1)}, u32[]{:S(2)}, u32[]{:S(2)}) collective-permute-start(f32[80,80]{1,0:T(8,128)S(1)} %bitcast.72), channel_id=1, source_target_pairs={{1,32},{2,64},{3,96},{4,128},{5,160},{6,192},{7,224},{8,256},{9,28... | collective-permute-start | bytes 76808 | tf_op jit(solution)/shard_map/ppermute | solution.py:76

commit v2 on v1

v2 whole, which is shorter than its diff:
```python
import jax
import jax.numpy as jnp
from jax import lax
from jax.sharding import PartitionSpec as P

AXES = ("ex", "par")
CHUNKS = 2
LANES = 128


def tile_of(rows_a, rows_b):
    return lax.dot_general(
        rows_a, rows_b, (((1,), (1,)), ((), ())), preferred_element_type=jnp.float32
    )


def shards(jacobian):
    ex_size, par_size = lax.axis_size("ex"), lax.axis_size("par")
    planes = ex_size // 2
    half = planes // 2
    position, column = lax.axis_index("ex"), lax.axis_index("par")
    plane, member, core = position // 2, position % 2, column % 2
    way = 1 - 2 * core
    rows, cols = jacobian.shape
    width = cols // CHUNKS
    swap = [(i, i ^ 1) for i in range(ex_size)]
    onward = [
        (i * par_size + p, ((i + (2 if p % 2 == 0 else -2)) % ex_size) * par_size + p)
        for i in range(ex_size)
        for p in range(par_size)
    ]

    def in_order(block_a, block_b):
        return jnp.where(
            member == 0,
            jnp.concatenate([block_a, block_b], 0),
            jnp.concatenate([block_b, block_a], 0),
        )

    def hop(block):
        return lax.ppermute(block, AXES, onward)

    strip = jnp.zeros((planes, rows, 2 * rows), jnp.bfloat16)

    def put(strip, travel, held, where):
        tile = sum(tile_of(block, block_held) for block, block_held in zip(travel, held))
        return lax.dynamic_update_slice_in_dim(
            strip, tile.astype(jnp.bfloat16)[None], jnp.mod(where, planes), 0
        )

    mine = [lax.slice_in_dim(jacobian, c * width, (c + 1) * width, axis=1) for c in range(CHUNKS)]
    own = [in_order(block, lax.ppermute(block, "ex", swap)) for block in mine]
    travel = list(mine)
    strip = put(strip, travel, own, plane)
    for step in range(1, half):
        travel = [hop(block) for block in travel]
        strip = put(strip, travel, own, plane - way * step)

    def side_of(block, side):
        return lax.dynamic_slice_in_dim(block, side * (width // 2), width // 2, 1)

    theirs_side = jnp.mod(plane + way, planes) // half
    travel = [hop(side_of(block, theirs_side)) for block in travel]
    held = [side_of(block, plane // half) for block in own]
    strip = put(strip, travel, held, plane + half)

    groups = [[e * par_size + p for p in range(par_size)] for e in range(ex_size)]
    parts = lax.all_to_all(strip, AXES, 0, 0, axis_index_groups=groups, tiled=True)
    total = jnp.sum(parts.astype(jnp.float32), axis=0)
    mirror = [
        ((2 * z + m) * par_size + p, (2 * p + m) * par_size + z)
        for z in range(planes)
        for m in range(2)
        for p in range(par_size)
        if p != z
    ]
    packed = total.reshape(rows * 2 * rows // LANES, LANES)
    added = lax.ppermute(packed, AXES, mirror).reshape(rows, 2 * rows)
    away = lax.dynamic_slice_in_dim(total, (1 - member) * rows, rows, 1)
    kept = lax.dynamic_slice_in_dim(total, member * rows, rows, 1)
    got = lax.ppermute(away, "ex", swap)
    return in_order(kept, got).T + added


def solution(mesh):
    return jax.shard_map(
        shards, mesh=mesh, in_specs=(P("ex", "par"),), out_specs=P("ex", "par"), check_vma=False
    )
```

time: 197 us -> 163 us (0.83)
  waiting for transfers between devices: 115 us -> 75.2 us
  matrix products: 6.94 us -> 15.1 us
  local copies, waits for them, and re-layouts: 8.59 us -> 3.4 us
    ppermute x19 -> x20, waiting for transfers between devices: 96.2 us -> 65.5 us  [the longest x16 56.9 us: hop(): return lax.ppermute(block, AXES, onward)]
    all_to_all x1, waiting for transfers between devices: 18.4 us -> 9.73 us  [shards(): lax.all_to_all(strip, AXES, 0, 0, axis_index_groups=groups, tiled=True)]
    dot_general x17 -> x18, matrix products: 6.94 us -> 15.1 us  [tile_of(): lax.dot_general(rows_a, rows_b, (((1,), (1,)), ((), ())), preferred_eleme...]
    dynamic_update_slice x9 -> x1, local copies, waits for them, and re-layouts: 5.81 us -> 0.63 us  [put(): lax.dynamic_update_slice_in_dim(strip, tile.astype(jnp.bfloat16)[None], j...]
    ppermute x19 -> x20, starting transfers between devices: 57.2 us -> 59.6 us  [the longest x16 34.4 us: hop(): return lax.ppermute(block, AXES, onward)]
  transfers between devices with their start and end apart: 20 -> 21, of which waited for: 20 -> 17; matrix products, arithmetic and copies ran while one was open for 7% -> 11% of each run, Pallas kernels for 0% -> 0%
where the time goes in v2:
time: 163 us; the launch traced here: 162 us
  waiting for transfers between devices  75.2 us (46%)
  starting transfers between devices  65.4 us (40%)
  matrix products  15.1 us (9%)
  local copies, waits for them, and re-layouts  3.4 us (2%)
  other arithmetic  2.73 us (2%)
    ppermute x16, waiting for transfers between devices, hop(): return lax.ppermute(block, AXES, onward)  56.9 us
    ppermute x16, starting transfers between devices, hop(): return lax.ppermute(block, AXES, onward)  34.4 us
    dot_general x18, matrix products, tile_of(): lax.dot_general(rows_a, rows_b, (((1,), (1,)), ((), ())), preferred_eleme...  15.1 us
    ppermute x1, starting transfers between devices, shards(): added = lax.ppermute(packed, AXES, mirror).reshape(rows, 2 * rows)  10.7 us
    ppermute x2, starting transfers between devices, shards(): own = [in_order(block, lax.ppermute(block, 'ex', swap)) for block in mine]  9.87 us
    all_to_all x1, waiting for transfers between devices, shards(): lax.all_to_all(strip, AXES, 0, 0, axis_index_groups=groups, tiled=True)  9.73 us
    ppermute x2, waiting for transfers between devices, shards(): own = [in_order(block, lax.ppermute(block, 'ex', swap)) for block in mine]  5.91 us
    all_to_all x1, starting transfers between devices, shards(): lax.all_to_all(strip, AXES, 0, 0, axis_index_groups=groups, tiled=True)  5.75 us
  transfers between devices with their start and end apart: 21, of which 17 were waited for; matrix products, arithmetic and copies ran while one was open for 11% of the time, Pallas kernels for 0%

profile of v2, /device:TPU:16, one launch (start us, length us, event | category | flops | bytes accessed | tf_op | source)
XLA Modules:
  0.0 162.4 jit_solution(12777770837090239681)
XLA Ops:
  1.4 3.8 %collective-permute-start.3 = (bf16[80,4096]{1,0:T(8,128)(2,1)S(1)}, bf16[80,4096]{1,0:T(8,128)(2,1)S(1)}, u32[]{:S(2)}, u32[]{:S(2)}) collective-permute-start(bf16[80,4096]{1,0:T(8,128)(2,1)S(1)} %get-tuple-element.6), channel_id=1, source_target_pairs={{0,32},{1,481},{2,34},{3,483},{4,36},{5,485},{6,38},{7,487},{8,40}... | collective-permute-start | bytes 1966088 | tf_op jit(solution)/shard_map/ppermute | solution.py:41
  5.2 3.8 %collective-permute-start.2 = (bf16[80,4096]{1,0:T(8,128)(2,1)S(1)}, bf16[80,4096]{1,0:T(8,128)(2,1)}, u32[]{:S(2)}, u32[]{:S(2)}) collective-permute-start(bf16[80,4096]{1,0:T(8,128)(2,1)S(1)} %get-tuple-element.5), channel_id=1, source_target_pairs={{0,32},{1,481},{2,34},{3,483},{4,36},{5,485},{6,38},{7,487},{8,40}... | collective-permute-start | bytes 1966088 | tf_op jit(solution)/shard_map/ppermute | solution.py:41
  9.1 4.9 %collective-permute-start.1 = (bf16[80,4096]{1,0:T(8,128)(2,1)S(1)}, bf16[80,4096]{1,0:T(8,128)(2,1)}, u32[]{:S(2)}, u32[]{:S(2)}) collective-permute-start(bf16[80,4096]{1,0:T(8,128)(2,1)S(1)} %get-tuple-element.6), channel_id=1, source_target_pairs={{0,16},{16,0},{32,48},{48,32},{64,80},{80,64},{96,112},{112,96},{1... | collective-permute-start | bytes 1966088 | tf_op jit(solution)/shard_map/ppermute | solution.py:52
  14.0 7.4 %collective-permute-done.3 = bf16[80,4096]{1,0:T(8,128)(2,1)S(1)} collective-permute-done((bf16[80,4096]{1,0:T(8,128)(2,1)S(1)}, bf16[80,4096]{1,0:T(8,128)(2,1)S(1)}, u32[]{:S(2)}, u32[]{:S(2)}) %collective-permute-start.3) | collective-permute-done | bytes 655392 | tf_op jit(solution)/shard_map/ppermute | solution.py:41
  21.4 1.9 %collective-permute-start.5 = (bf16[80,4096]{1,0:T(8,128)(2,1)S(1)}, bf16[80,4096]{1,0:T(8,128)(2,1)S(1)}, u32[]{:S(2)}, u32[]{:S(2)}) collective-permute-start(bf16[80,4096]{1,0:T(8,128)(2,1)S(1)} %collective-permute-done.3), channel_id=1, source_target_pairs={{0,32},{1,481},{2,34},{3,483},{4,36},{5,485},{6,38},{7,487},{8,40}... | collective-permute-start | bytes 1966088 | tf_op jit(solution)/shard_map/ppermute | solution.py:41
  23.3 4.9 %collective-permute-start = (bf16[80,4096]{1,0:T(8,128)(2,1)S(1)}, bf16[80,4096]{1,0:T(8,128)(2,1)S(1)}, u32[]{:S(2)}, u32[]{:S(2)}) collective-permute-start(bf16[80,4096]{1,0:T(8,128)(2,1)S(1)} %get-tuple-element.5), channel_id=1, source_target_pairs={{0,16},{16,0},{32,48},{48,32},{64,80},{80,64},{96,112},{112,96},{1... | collective-permute-start | bytes 1966088 | tf_op jit(solution)/shard_map/ppermute | solution.py:52
  28.5 1.9 %collective-permute-start.4 = (bf16[80,4096]{1,0:T(8,128)(2,1)}, bf16[80,4096]{1,0:T(8,128)(2,1)S(1)}, u32[]{:S(2)}, u32[]{:S(2)}) collective-permute-start(bf16[80,4096]{1,0:T(8,128)(2,1)} %collective-permute-done.2), channel_id=1, source_target_pairs={{0,32},{1,481},{2,34},{3,483},{4,36},{5,485},{6,38},{7,487},{8,40}... | collective-permute-start | bytes 1966088 | tf_op jit(solution)/shard_map/ppermute | solution.py:41
  32.0 3.4 %collective-permute-done.5 = bf16[80,4096]{1,0:T(8,128)(2,1)S(1)} collective-permute-done((bf16[80,4096]{1,0:T(8,128)(2,1)S(1)}, bf16[80,4096]{1,0:T(8,128)(2,1)S(1)}, u32[]{:S(2)}, u32[]{:S(2)}) %collective-permute-start.5) | collective-permute-done | bytes 655392 | tf_op jit(solution)/shard_map/ppermute | solution.py:41
  35.4 1.9 %collective-permute-start.7 = (bf16[80,4096]{1,0:T(8,128)(2,1)S(1)}, bf16[80,4096]{1,0:T(8,128)(2,1)S(1)}, u32[]{:S(2)}, u32[]{:S(2)}) collective-permute-start(bf16[80,4096]{1,0:T(8,128)(2,1)S(1)} %collective-permute-done.5), channel_id=1, source_target_pairs={{0,32},{1,481},{2,34},{3,483},{4,36},{5,485},{6,38},{7,487},{8,40}... | collective-permute-start | bytes 1966088 | tf_op jit(solution)/shard_map/ppermute | solution.py:41
  37.3 5.9 %collective-permute-done = bf16[80,4096]{1,0:T(8,128)(2,1)S(1)} collective-permute-done((bf16[80,4096]{1,0:T(8,128)(2,1)S(1)}, bf16[80,4096]{1,0:T(8,128)(2,1)S(1)}, u32[]{:S(2)}, u32[]{:S(2)}) %collective-permute-start) | collective-permute-done | bytes 655392 | tf_op jit(solution)/shard_map/ppermute | solution.py:52
  43.5 1.9 %collective-permute-start.6 = (bf16[80,4096]{1,0:T(8,128)(2,1)S(1)}, bf16[80,4096]{1,0:T(8,128)(2,1)S(1)}, u32[]{:S(2)}, u32[]{:S(2)}) collective-permute-start(bf16[80,4096]{1,0:T(8,128)(2,1)S(1)} %collective-permute-done.4), channel_id=1, source_target_pairs={{0,32},{1,481},{2,34},{3,483},{4,36},{5,485},{6,38},{7,487},{8,40}... | collective-permute-start | bytes 1966088 | tf_op jit(solution)/shard_map/ppermute | solution.py:41
  49.5 1.9 %collective-permute-start.9 = (bf16[80,4096]{1,0:T(8,128)(2,1)S(1)}, bf16[80,4096]{1,0:T(8,128)(2,1)S(1)}, u32[]{:S(2)}, u32[]{:S(2)}) collective-permute-start(bf16[80,4096]{1,0:T(8,128)(2,1)S(1)} %collective-permute-done.7), channel_id=1, source_target_pairs={{0,32},{1,481},{2,34},{3,483},{4,36},{5,485},{6,38},{7,487},{8,40}... | collective-permute-start | bytes 1966088 | tf_op jit(solution)/shard_map/ppermute | solution.py:41
  51.9 8.4 %collective-permute-done.6 = bf16[80,4096]{1,0:T(8,128)(2,1)S(1)} collective-permute-done((bf16[80,4096]{1,0:T(8,128)(2,1)S(1)}, bf16[80,4096]{1,0:T(8,128)(2,1)S(1)}, u32[]{:S(2)}, u32[]{:S(2)}) %collective-permute-start.6) | collective-permute-done | bytes 655392 | tf_op jit(solution)/shard_map/ppermute | solution.py:41
  62.2 2.2 %fusion.23 = bf16[16,80,160]{1,2,0:T(8,128)(2,1)} fusion(bf16[16,80,160]{1,2,0:T(8,128)(2,1)} %fusion.25, s32[]{:T(128)S(6)} %select_n.133, f32[160,80]{1,0:T(8,128)S(1)} %fusion.37, bf16[80,4096]{1,0:T(8,128)(2,1)} %collective-permute-done.2, bf16[80,4096]{1,0:T(8,128)(2,1)S(1)} %collective-permute-done, bf16[80,4096]{1,0:T(8,128)(2,1)S(1)} %get-tuple-element.5, ...), kind=kOutput, calls=%fused_computation.35 | convolution fusion | flops 110781440 | bytes 2058245 | tf_op jit(solution)/shard_map/dot_general | solution.py:12
  64.9 2.4 %collective-permute-done.9 = bf16[80,4096]{1,0:T(8,128)(2,1)S(1)} collective-permute-done((bf16[80,4096]{1,0:T(8,128)(2,1)S(1)}, bf16[80,4096]{1,0:T(8,128)(2,1)S(1)}, u32[]{:S(2)}, u32[]{:S(2)}) %collective-permute-start.9) | collective-permute-done | bytes 655392 | tf_op jit(solution)/shard_map/ppermute | solution.py:41
  70.4 3.9 %collective-permute-done.8 = bf16[80,4096]{1,0:T(8,128)(2,1)S(1)} collective-permute-done((bf16[80,4096]{1,0:T(8,128)(2,1)S(1)}, bf16[80,4096]{1,0:T(8,128)(2,1)S(1)}, u32[]{:S(2)}, u32[]{:S(2)}) %collective-permute-start.8) | collective-permute-done | bytes 655392 | tf_op jit(solution)/shard_map/ppermute | solution.py:41
  74.3 1.9 %collective-permute-start.10 = (bf16[80,4096]{1,0:T(8,128)(2,1)S(1)}, bf16[80,4096]{1,0:T(8,128)(2,1)S(1)}, u32[]{:S(2)}, u32[]{:S(2)}) collective-permute-start(bf16[80,4096]{1,0:T(8,128)(2,1)S(1)} %collective-permute-done.8), channel_id=1, source_target_pairs={{0,32},{1,481},{2,34},{3,483},{4,36},{5,485},{6,38},{7,487},{8,40}... | collective-permute-start | bytes 1966088 | tf_op jit(solution)/shard_map/ppermute | solution.py:41
  77.9 3.4 %collective-permute-done.11 = bf16[80,4096]{1,0:T(8,128)(2,1)S(1)} collective-permute-done((bf16[80,4096]{1,0:T(8,128)(2,1)S(1)}, bf16[80,4096]{1,0:T(8,128)(2,1)S(1)}, u32[]{:S(2)}, u32[]{:S(2)}) %collective-permute-start.11) | collective-permute-done | bytes 655392 | tf_op jit(solution)/shard_map/ppermute | solution.py:41
  83.8 4.6 %collective-permute-done.10 = bf16[80,4096]{1,0:T(8,128)(2,1)S(1)} collective-permute-done((bf16[80,4096]{1,0:T(8,128)(2,1)S(1)}, bf16[80,4096]{1,0:T(8,128)(2,1)S(1)}, u32[]{:S(2)}, u32[]{:S(2)}) %collective-permute-start.10) | collective-permute-done | bytes 655392 | tf_op jit(solution)/shard_map/ppermute | solution.py:41
  91.9 3.4 %collective-permute-done.13 = bf16[80,4096]{1,0:T(8,128)(2,1)S(1)} collective-permute-done((bf16[80,4096]{1,0:T(8,128)(2,1)S(1)}, bf16[80,4096]{1,0:T(8,128)(2,1)S(1)}, u32[]{:S(2)}, u32[]{:S(2)}) %collective-permute-start.13) | collective-permute-done | bytes 655392 | tf_op jit(solution)/shard_map/ppermute | solution.py:41
  95.4 1.9 %collective-permute-start.15 = (bf16[80,4096]{1,0:T(8,128)(2,1)S(1)}, bf16[80,4096]{1,0:T(8,128)(2,1)S(1)}, u32[]{:S(2)}, u32[]{:S(2)}) collective-permute-start(bf16[80,4096]{1,0:T(8,128)(2,1)S(1)} %collective-permute-done.13), channel_id=1, source_target_pairs={{0,32},{1,481},{2,34},{3,483},{4,36},{5,485},{6,38},{7,487},{8,40}... | collective-permute-start | bytes 1966088 | tf_op jit(solution)/shard_map/ppermute | solution.py:41
  98.4 3.9 %collective-permute-done.12 = bf16[80,4096]{1,0:T(8,128)(2,1)S(1)} collective-permute-done((bf16[80,4096]{1,0:T(8,128)(2,1)S(1)}, bf16[80,4096]{1,0:T(8,128)(2,1)S(1)}, u32[]{:S(2)}, u32[]{:S(2)}) %collective-permute-start.12) | collective-permute-done | bytes 655392 | tf_op jit(solution)/shard_map/ppermute | solution.py:41
  102.4 1.9 %collective-permute-start.14 = (bf16[80,4096]{1,0:T(8,128)(2,1)S(1)}, bf16[80,4096]{1,0:T(8,128)(2,1)S(1)}, u32[]{:S(2)}, u32[]{:S(2)}) collective-permute-start(bf16[80,4096]{1,0:T(8,128)(2,1)S(1)} %collective-permute-done.12), channel_id=1, source_target_pairs={{0,32},{1,481},{2,34},{3,483},{4,36},{5,485},{6,38},{7,487},{8,40}... | collective-permute-start | bytes 1966088 | tf_op jit(solution)/shard_map/ppermute | solution.py:41
  106.0 3.4 %collective-permute-done.15 = bf16[80,4096]{1,0:T(8,128)(2,1)S(1)} collective-permute-done((bf16[80,4096]{1,0:T(8,128)(2,1)S(1)}, bf16[80,4096]{1,0:T(8,128)(2,1)S(1)}, u32[]{:S(2)}, u32[]{:S(2)}) %collective-permute-start.15) | collective-permute-done | bytes 655392 | tf_op jit(solution)/shard_map/ppermute | solution.py:41
  109.4 1.9 %collective-permute-start.17 = (bf16[80,2048]{1,0:T(8,128)(2,1)S(1)}, bf16[80,2048]{1,0:T(8,128)(2,1)S(1)}, u32[]{:S(2)}, u32[]{:S(2)}) collective-permute-start(bf16[80,2048]{1,0:T(8,128)(2,1)S(1)} %constant_dynamic-slice_fusion.2), channel_id=1, source_target_pairs={{0,32},{1,481},{2,34},{3,483},{4,36},{5,485},{6,38},{7,487},{8,40}... | collective-permute-start | bytes 983048 | tf_op jit(solution)/shard_map/ppermute | solution.py:41
  111.4 5.1 %collective-permute-done.14 = bf16[80,4096]{1,0:T(8,128)(2,1)S(1)} collective-permute-done((bf16[80,4096]{1,0:T(8,128)(2,1)S(1)}, bf16[80,4096]{1,0:T(8,128)(2,1)S(1)}, u32[]{:S(2)}, u32[]{:S(2)}) %collective-permute-start.14) | collective-permute-done | bytes 655392 | tf_op jit(solution)/shard_map/ppermute | solution.py:41
  116.5 1.9 %collective-permute-start.16 = (bf16[80,2048]{1,0:T(8,128)(2,1)S(1)}, bf16[80,2048]{1,0:T(8,128)(2,1)S(1)}, u32[]{:S(2)}, u32[]{:S(2)}) collective-permute-start(bf16[80,2048]{1,0:T(8,128)(2,1)S(1)} %constant_dynamic-slice_fusion.3), channel_id=1, source_target_pairs={{0,32},{1,481},{2,34},{3,483},{4,36},{5,485},{6,38},{7,487},{8,40}... | collective-permute-start | bytes 983048 | tf_op jit(solution)/shard_map/ppermute | solution.py:41
  120.4 6.2 %collective-permute-done.16 = bf16[80,2048]{1,0:T(8,128)(2,1)S(1)} collective-permute-done((bf16[80,2048]{1,0:T(8,128)(2,1)S(1)}, bf16[80,2048]{1,0:T(8,128)(2,1)S(1)}, u32[]{:S(2)}, u32[]{:S(2)}) %collective-permute-start.16) | collective-permute-done | bytes 327712 | tf_op jit(solution)/shard_map/ppermute | solution.py:41
  127.7 5.8 %all-to-all-start = ((bf16[16,80,160]{1,2,0:T(8,128)(2,1)}), bf16[16,80,160]{1,2,0:T(8,128)(2,1)S(1)}, u32[]{:S(2)}, u32[]{:S(2)}) async-start(bf16[16,80,160]{1,2,0:T(8,128)(2,1)} %constant_dynamic-update-slice_fusion), calls=%async_computation | async-start | bytes 1310720 | tf_op jit(solution)/shard_map/all_to_all | solution.py:68
  133.5 9.7 %all-to-all-done = bf16[16,80,160]{1,2,0:T(8,128)(2,1)S(1)} async-done(((bf16[16,80,160]{1,2,0:T(8,128)(2,1)}), bf16[16,80,160]{1,2,0:T(8,128)(2,1)S(1)}, u32[]{:S(2)}, u32[]{:S(2)}) %all-to-all-start) | async-done | bytes 409632 | tf_op jit(solution)/shard_map/all_to_all | solution.py:68
  143.5 10.7 %collective-permute-start.19 = (f32[100,128]{1,0:T(8,128)S(1)}, f32[100,128]{1,0:T(8,128)S(1)}, u32[]{:S(2)}, u32[]{:S(2)}) collective-permute-start(f32[100,128]{1,0:T(8,128)S(1)} %reshape.6), channel_id=1, source_target_pairs={{1,32},{2,64},{3,96},{4,128},{5,160},{6,192},{7,224},{8,256},{9,28... | collective-permute-start | bytes 153608 | tf_op jit(solution)/shard_map/ppermute | solution.py:78
  154.3 4.6 %collective-permute-start.18 = (f32[80,80]{0,1:T(8,128)S(1)}, f32[80,80]{0,1:T(8,128)S(1)}, u32[]{:S(2)}, u32[]{:S(2)}) collective-permute-start(f32[80,80]{0,1:T(8,128)S(1)} %get-tuple-element.8), channel_id=1, source_target_pairs={{0,16},{16,0},{32,48},{48,32},{64,80},{80,64},{96,112},{112,96},{1... | collective-permute-start | bytes 76808 | tf_op jit(solution)/shard_map/ppermute | solution.py:81
  (44 shorter events, 30.7 us)
Async XLA Ops:
  1.4 20.0 %collective-permute-start.3 = (bf16[80,4096]{1,0:T(8,128)(2,1)S(1)}, bf16[80,4096]{1,0:T(8,128)(2,1)S(1)}, u32[]{:S(2)}, u32[]{:S(2)}) collective-permute-start(bf16[80,4096]{1,0:T(8,128)(2,1)S(1)} %get-tuple-element.6), channel_id=1, source_target_pairs={{0,32},{1,481},{2,34},{3,483},{4,36},{5,485},{6,38},{7,487},{8,40}... | collective-permute-start | bytes 1966088 | tf_op jit(solution)/shard_map/ppermute | solution.py:41
  5.2 23.3 %collective-permute-start.2 = (bf16[80,4096]{1,0:T(8,128)(2,1)S(1)}, bf16[80,4096]{1,0:T(8,128)(2,1)}, u32[]{:S(2)}, u32[]{:S(2)}) collective-permute-start(bf16[80,4096]{1,0:T(8,128)(2,1)S(1)} %get-tuple-element.5), channel_id=1, source_target_pairs={{0,32},{1,481},{2,34},{3,483},{4,36},{5,485},{6,38},{7,487},{8,40}... | collective-permute-start | bytes 1966088 | tf_op jit(solution)/shard_map/ppermute | solution.py:41
  9.1 21.4 %collective-permute-start.1 = (bf16[80,4096]{1,0:T(8,128)(2,1)S(1)}, bf16[80,4096]{1,0:T(8,128)(2,1)}, u32[]{:S(2)}, u32[]{:S(2)}) collective-permute-start(bf16[80,4096]{1,0:T(8,128)(2,1)S(1)} %get-tuple-element.6), channel_id=1, source_target_pairs={{0,16},{16,0},{32,48},{48,32},{64,80},{80,64},{96,112},{112,96},{1... | collective-permute-start | bytes 1966088 | tf_op jit(solution)/shard_map/ppermute | solution.py:52
  21.4 14.0 %collective-permute-start.5 = (bf16[80,4096]{1,0:T(8,128)(2,1)S(1)}, bf16[80,4096]{1,0:T(8,128)(2,1)S(1)}, u32[]{:S(2)}, u32[]{:S(2)}) collective-permute-start(bf16[80,4096]{1,0:T(8,128)(2,1)S(1)} %collective-permute-done.3), channel_id=1, source_target_pairs={{0,32},{1,481},{2,34},{3,483},{4,36},{5,485},{6,38},{7,487},{8,40}... | collective-permute-start | bytes 1966088 | tf_op jit(solution)/shard_map/ppermute | solution.py:41
  23.3 20.0 %collective-permute-start = (bf16[80,4096]{1,0:T(8,128)(2,1)S(1)}, bf16[80,4096]{1,0:T(8,128)(2,1)S(1)}, u32[]{:S(2)}, u32[]{:S(2)}) collective-permute-start(bf16[80,4096]{1,0:T(8,128)(2,1)S(1)} %get-tuple-element.5), channel_id=1, source_target_pairs={{0,16},{16,0},{32,48},{48,32},{64,80},{80,64},{96,112},{112,96},{1... | collective-permute-start | bytes 1966088 | tf_op jit(solution)/shard_map/ppermute | solution.py:52
  28.5 15.0 %collective-permute-start.4 = (bf16[80,4096]{1,0:T(8,128)(2,1)}, bf16[80,4096]{1,0:T(8,128)(2,1)S(1)}, u32[]{:S(2)}, u32[]{:S(2)}) collective-permute-start(bf16[80,4096]{1,0:T(8,128)(2,1)} %collective-permute-done.2), channel_id=1, source_target_pairs={{0,32},{1,481},{2,34},{3,483},{4,36},{5,485},{6,38},{7,487},{8,40}... | collective-permute-start | bytes 1966088 | tf_op jit(solution)/shard_map/ppermute | solution.py:41
  32.0 13.4 %copy-start = (bf16[80,8192]{1,0:T(8,128)(2,1)S(1)}, bf16[80,8192]{1,0:T(8,128)(2,1)}, u32[]{:S(2)}) copy-start(bf16[80,8192]{1,0:T(8,128)(2,1)} %param.1) | copy-start | bytes 3932164
  35.4 14.0 %collective-permute-start.7 = (bf16[80,4096]{1,0:T(8,128)(2,1)S(1)}, bf16[80,4096]{1,0:T(8,128)(2,1)S(1)}, u32[]{:S(2)}, u32[]{:S(2)}) collective-permute-start(bf16[80,4096]{1,0:T(8,128)(2,1)S(1)} %collective-permute-done.5), channel_id=1, source_target_pairs={{0,32},{1,481},{2,34},{3,483},{4,36},{5,485},{6,38},{7,487},{8,40}... | collective-permute-start | bytes 1966088 | tf_op jit(solution)/shard_map/ppermute | solution.py:41
  43.5 16.7 %collective-permute-start.6 = (bf16[80,4096]{1,0:T(8,128)(2,1)S(1)}, bf16[80,4096]{1,0:T(8,128)(2,1)S(1)}, u32[]{:S(2)}, u32[]{:S(2)}) collective-permute-start(bf16[80,4096]{1,0:T(8,128)(2,1)S(1)} %collective-permute-done.4), channel_id=1, source_target_pairs={{0,32},{1,481},{2,34},{3,483},{4,36},{5,485},{6,38},{7,487},{8,40}... | collective-permute-start | bytes 1966088 | tf_op jit(solution)/shard_map/ppermute | solution.py:41
  49.5 17.8 %collective-permute-start.9 = (bf16[80,4096]{1,0:T(8,128)(2,1)S(1)}, bf16[80,4096]{1,0:T(8,128)(2,1)S(1)}, u32[]{:S(2)}, u32[]{:S(2)}) collective-permute-start(bf16[80,4096]{1,0:T(8,128)(2,1)S(1)} %collective-permute-done.7), channel_id=1, source_target_pairs={{0,32},{1,481},{2,34},{3,483},{4,36},{5,485},{6,38},{7,487},{8,40}... | collective-permute-start | bytes 1966088 | tf_op jit(solution)/shard_map/ppermute | solution.py:41
  60.3 14.0 %collective-permute-start.8 = (bf16[80,4096]{1,0:T(8,128)(2,1)S(1)}, bf16[80,4096]{1,0:T(8,128)(2,1)S(1)}, u32[]{:S(2)}, u32[]{:S(2)}) collective-permute-start(bf16[80,4096]{1,0:T(8,128)(2,1)S(1)} %collective-permute-done.6), channel_id=1, source_target_pairs={{0,32},{1,481},{2,34},{3,483},{4,36},{5,485},{6,38},{7,487},{8,40}... | collective-permute-start | bytes 1966088 | tf_op jit(solution)/shard_map/ppermute | solution.py:41
  67.3 14.0 %collective-permute-start.11 = (bf16[80,4096]{1,0:T(8,128)(2,1)S(1)}, bf16[80,4096]{1,0:T(8,128)(2,1)S(1)}, u32[]{:S(2)}, u32[]{:S(2)}) collective-permute-start(bf16[80,4096]{1,0:T(8,128)(2,1)S(1)} %collective-permute-done.9), channel_id=1, source_target_pairs={{0,32},{1,481},{2,34},{3,483},{4,36},{5,485},{6,38},{7,487},{8,40}... | collective-permute-start | bytes 1966088 | tf_op jit(solution)/shard_map/ppermute | solution.py:41
  74.3 14.0 %collective-permute-start.10 = (bf16[80,4096]{1,0:T(8,128)(2,1)S(1)}, bf16[80,4096]{1,0:T(8,128)(2,1)S(1)}, u32[]{:S(2)}, u32[]{:S(2)}) collective-permute-start(bf16[80,4096]{1,0:T(8,128)(2,1)S(1)} %collective-permute-done.8), channel_id=1, source_target_pairs={{0,32},{1,481},{2,34},{3,483},{4,36},{5,485},{6,38},{7,487},{8,40}... | collective-permute-start | bytes 1966088 | tf_op jit(solution)/shard_map/ppermute | solution.py:41
  81.3 14.0 %collective-permute-start.13 = (bf16[80,4096]{1,0:T(8,128)(2,1)S(1)}, bf16[80,4096]{1,0:T(8,128)(2,1)S(1)}, u32[]{:S(2)}, u32[]{:S(2)}) collective-permute-start(bf16[80,4096]{1,0:T(8,128)(2,1)S(1)} %collective-permute-done.11), channel_id=1, source_target_pairs={{0,32},{1,481},{2,34},{3,483},{4,36},{5,485},{6,38},{7,487},{8,40}... | collective-permute-start | bytes 1966088 | tf_op jit(solution)/shard_map/ppermute | solution.py:41
  88.3 14.0 %collective-permute-start.12 = (bf16[80,4096]{1,0:T(8,128)(2,1)S(1)}, bf16[80,4096]{1,0:T(8,128)(2,1)S(1)}, u32[]{:S(2)}, u32[]{:S(2)}) collective-permute-start(bf16[80,4096]{1,0:T(8,128)(2,1)S(1)} %collective-permute-done.10), channel_id=1, source_target_pairs={{0,32},{1,481},{2,34},{3,483},{4,36},{5,485},{6,38},{7,487},{8,40}... | collective-permute-start | bytes 1966088 | tf_op jit(solution)/shard_map/ppermute | solution.py:41
  95.4 14.0 %collective-permute-start.15 = (bf16[80,4096]{1,0:T(8,128)(2,1)S(1)}, bf16[80,4096]{1,0:T(8,128)(2,1)S(1)}, u32[]{:S(2)}, u32[]{:S(2)}) collective-permute-start(bf16[80,4096]{1,0:T(8,128)(2,1)S(1)} %collective-permute-done.13), channel_id=1, source_target_pairs={{0,32},{1,481},{2,34},{3,483},{4,36},{5,485},{6,38},{7,487},{8,40}... | collective-permute-start | bytes 1966088 | tf_op jit(solution)/shard_map/ppermute | solution.py:41
  102.4 14.0 %collective-permute-start.14 = (bf16[80,4096]{1,0:T(8,128)(2,1)S(1)}, bf16[80,4096]{1,0:T(8,128)(2,1)S(1)}, u32[]{:S(2)}, u32[]{:S(2)}) collective-permute-start(bf16[80,4096]{1,0:T(8,128)(2,1)S(1)} %collective-permute-done.12), channel_id=1, source_target_pairs={{0,32},{1,481},{2,34},{3,483},{4,36},{5,485},{6,38},{7,487},{8,40}... | collective-permute-start | bytes 1966088 | tf_op jit(solution)/shard_map/ppermute | solution.py:41
  109.4 10.6 %collective-permute-start.17 = (bf16[80,2048]{1,0:T(8,128)(2,1)S(1)}, bf16[80,2048]{1,0:T(8,128)(2,1)S(1)}, u32[]{:S(2)}, u32[]{:S(2)}) collective-permute-start(bf16[80,2048]{1,0:T(8,128)(2,1)S(1)} %constant_dynamic-slice_fusion.2), channel_id=1, source_target_pairs={{0,32},{1,481},{2,34},{3,483},{4,36},{5,485},{6,38},{7,487},{8,40}... | collective-permute-start | bytes 983048 | tf_op jit(solution)/shard_map/ppermute | solution.py:41
  116.5 10.2 %collective-permute-start.16 = (bf16[80,2048]{1,0:T(8,128)(2,1)S(1)}, bf16[80,2048]{1,0:T(8,128)(2,1)S(1)}, u32[]{:S(2)}, u32[]{:S(2)}) collective-permute-start(bf16[80,2048]{1,0:T(8,128)(2,1)S(1)} %constant_dynamic-slice_fusion.3), channel_id=1, source_target_pairs={{0,32},{1,481},{2,34},{3,483},{4,36},{5,485},{6,38},{7,487},{8,40}... | collective-permute-start | bytes 983048 | tf_op jit(solution)/shard_map/ppermute | solution.py:41
  127.7 15.5 %all-to-all-start = ((bf16[16,80,160]{1,2,0:T(8,128)(2,1)}), bf16[16,80,160]{1,2,0:T(8,128)(2,1)S(1)}, u32[]{:S(2)}, u32[]{:S(2)}) async-start(bf16[16,80,160]{1,2,0:T(8,128)(2,1)} %constant_dynamic-update-slice_fusion), calls=%async_computation | async-start | bytes 1310720 | tf_op jit(solution)/shard_map/all_to_all | solution.py:68
  143.5 17.1 %collective-permute-start.19 = (f32[100,128]{1,0:T(8,128)S(1)}, f32[100,128]{1,0:T(8,128)S(1)}, u32[]{:S(2)}, u32[]{:S(2)}) collective-permute-start(f32[100,128]{1,0:T(8,128)S(1)} %reshape.6), channel_id=1, source_target_pairs={{1,32},{2,64},{3,96},{4,128},{5,160},{6,192},{7,224},{8,256},{9,28... | collective-permute-start | bytes 153608 | tf_op jit(solution)/shard_map/ppermute | solution.py:78
  154.3 7.4 %collective-permute-start.18 = (f32[80,80]{0,1:T(8,128)S(1)}, f32[80,80]{0,1:T(8,128)S(1)}, u32[]{:S(2)}, u32[]{:S(2)}) collective-permute-start(f32[80,80]{0,1:T(8,128)S(1)} %get-tuple-element.8), channel_id=1, source_target_pairs={{0,16},{16,0},{32,48},{48,32},{64,80},{80,64},{96,112},{112,96},{1... | collective-permute-start | bytes 76808 | tf_op jit(solution)/shard_map/ppermute | solution.py:81

commit v3 on v2

--- a/solution.py
+++ b/solution.py
@@ -74,8 +74,7 @@
         for p in range(par_size)
         if p != z
     ]
-    packed = total.reshape(rows * 2 * rows // LANES, LANES)
-    added = lax.ppermute(packed, AXES, mirror).reshape(rows, 2 * rows)
+    added = lax.ppermute(total, AXES, mirror)
     away = lax.dynamic_slice_in_dim(total, (1 - member) * rows, rows, 1)
     kept = lax.dynamic_slice_in_dim(total, member * rows, rows, 1)
     got = lax.ppermute(away, "ex", swap)

time: 163 us -> 164 us (level)
  the two profiles are of different devices: /device:TPU:16 before, /device:TPU:31 now
where the time goes in v3:
time: 164 us; the launch traced here: 163 us
  starting transfers between devices  105 us (64%)
  waiting for transfers between devices  35.7 us (22%)
  matrix products  15.1 us (9%)
  local copies, waits for them, and re-layouts  4.01 us (2%)
  other arithmetic  1.99 us (1%)
    ppermute x16, starting transfers between devices, hop(): return lax.ppermute(block, AXES, onward)  82.7 us
    dot_general x18, matrix products, tile_of(): lax.dot_general(rows_a, rows_b, (((1,), (1,)), ((), ())), preferred_eleme...  15.1 us
    ppermute x16, waiting for transfers between devices, hop(): return lax.ppermute(block, AXES, onward)  11.7 us
    all_to_all x1, waiting for transfers between devices, shards(): lax.all_to_all(strip, AXES, 0, 0, axis_index_groups=groups, tiled=True)  8.87 us
    all_to_all x1, starting transfers between devices, shards(): lax.all_to_all(strip, AXES, 0, 0, axis_index_groups=groups, tiled=True)  8.11 us
    ppermute x1, waiting for transfers between devices, shards(): added = lax.ppermute(total, AXES, mirror)  7.14 us
    ppermute x2, starting transfers between devices, shards(): own = [in_order(block, lax.ppermute(block, 'ex', swap)) for block in mine]  5.91 us
    ppermute x1, starting transfers between devices, shards(): added = lax.ppermute(total, AXES, mirror)  5.63 us
  transfers between devices with their start and end apart: 21, of which 14 were waited for; matrix products, arithmetic and copies ran while one was open for 11% of the time, Pallas kernels for 0%

profile of v3, /device:TPU:31, one launch (start us, length us, event | category | flops | bytes accessed | tf_op | source)
XLA Modules:
  0.0 162.8 jit_solution(5934497633241624022)
XLA Ops:
  1.4 11.1 %collective-permute-start.3 = (bf16[80,4096]{1,0:T(8,128)(2,1)S(1)}, bf16[80,4096]{1,0:T(8,128)(2,1)S(1)}, u32[]{:S(2)}, u32[]{:S(2)}) collective-permute-start(bf16[80,4096]{1,0:T(8,128)(2,1)S(1)} %get-tuple-element.6), channel_id=1, source_target_pairs={{0,32},{1,481},{2,34},{3,483},{4,36},{5,485},{6,38},{7,487},{8,40}... | collective-permute-start | bytes 1966088 | tf_op jit(solution)/shard_map/ppermute | solution.py:41
  12.5 2.6 %collective-permute-start.2 = (bf16[80,4096]{1,0:T(8,128)(2,1)S(1)}, bf16[80,4096]{1,0:T(8,128)(2,1)}, u32[]{:S(2)}, u32[]{:S(2)}) collective-permute-start(bf16[80,4096]{1,0:T(8,128)(2,1)S(1)} %get-tuple-element.5), channel_id=1, source_target_pairs={{0,32},{1,481},{2,34},{3,483},{4,36},{5,485},{6,38},{7,487},{8,40}... | collective-permute-start | bytes 1966088 | tf_op jit(solution)/shard_map/ppermute | solution.py:41
  15.2 3.0 %collective-permute-start.1 = (bf16[80,4096]{1,0:T(8,128)(2,1)S(1)}, bf16[80,4096]{1,0:T(8,128)(2,1)}, u32[]{:S(2)}, u32[]{:S(2)}) collective-permute-start(bf16[80,4096]{1,0:T(8,128)(2,1)S(1)} %get-tuple-element.6), channel_id=1, source_target_pairs={{0,16},{16,0},{32,48},{48,32},{64,80},{80,64},{96,112},{112,96},{1... | collective-permute-start | bytes 1966088 | tf_op jit(solution)/shard_map/ppermute | solution.py:52
  18.2 1.8 %collective-permute-done.3 = bf16[80,4096]{1,0:T(8,128)(2,1)S(1)} collective-permute-done((bf16[80,4096]{1,0:T(8,128)(2,1)S(1)}, bf16[80,4096]{1,0:T(8,128)(2,1)S(1)}, u32[]{:S(2)}, u32[]{:S(2)}) %collective-permute-start.3) | collective-permute-done | bytes 655392 | tf_op jit(solution)/shard_map/ppermute | solution.py:41
  20.0 5.4 %collective-permute-start.5 = (bf16[80,4096]{1,0:T(8,128)(2,1)S(1)}, bf16[80,4096]{1,0:T(8,128)(2,1)S(1)}, u32[]{:S(2)}, u32[]{:S(2)}) collective-permute-start(bf16[80,4096]{1,0:T(8,128)(2,1)S(1)} %collective-permute-done.3), channel_id=1, source_target_pairs={{0,32},{1,481},{2,34},{3,483},{4,36},{5,485},{6,38},{7,487},{8,40}... | collective-permute-start | bytes 1966088 | tf_op jit(solution)/shard_map/ppermute | solution.py:41
  25.5 2.9 %collective-permute-start = (bf16[80,4096]{1,0:T(8,128)(2,1)S(1)}, bf16[80,4096]{1,0:T(8,128)(2,1)S(1)}, u32[]{:S(2)}, u32[]{:S(2)}) collective-permute-start(bf16[80,4096]{1,0:T(8,128)(2,1)S(1)} %get-tuple-element.5), channel_id=1, source_target_pairs={{0,16},{16,0},{32,48},{48,32},{64,80},{80,64},{96,112},{112,96},{1... | collective-permute-start | bytes 1966088 | tf_op jit(solution)/shard_map/ppermute | solution.py:52
  28.6 3.8 %collective-permute-start.4 = (bf16[80,4096]{1,0:T(8,128)(2,1)}, bf16[80,4096]{1,0:T(8,128)(2,1)S(1)}, u32[]{:S(2)}, u32[]{:S(2)}) collective-permute-start(bf16[80,4096]{1,0:T(8,128)(2,1)} %collective-permute-done.2), channel_id=1, source_target_pairs={{0,32},{1,481},{2,34},{3,483},{4,36},{5,485},{6,38},{7,487},{8,40}... | collective-permute-start | bytes 1966088 | tf_op jit(solution)/shard_map/ppermute | solution.py:41
  32.5 1.6 maximum_select_fusion.1
  34.1 5.6 %collective-permute-start.7 = (bf16[80,4096]{1,0:T(8,128)(2,1)S(1)}, bf16[80,4096]{1,0:T(8,128)(2,1)S(1)}, u32[]{:S(2)}, u32[]{:S(2)}) collective-permute-start(bf16[80,4096]{1,0:T(8,128)(2,1)S(1)} %collective-permute-done.5), channel_id=1, source_target_pairs={{0,32},{1,481},{2,34},{3,483},{4,36},{5,485},{6,38},{7,487},{8,40}... | collective-permute-start | bytes 1966088 | tf_op jit(solution)/shard_map/ppermute | solution.py:41
  39.7 4.6 %collective-permute-done = bf16[80,4096]{1,0:T(8,128)(2,1)S(1)} collective-permute-done((bf16[80,4096]{1,0:T(8,128)(2,1)S(1)}, bf16[80,4096]{1,0:T(8,128)(2,1)S(1)}, u32[]{:S(2)}, u32[]{:S(2)}) %collective-permute-start) | collective-permute-done | bytes 655392 | tf_op jit(solution)/shard_map/ppermute | solution.py:52
  44.6 7.1 %collective-permute-start.6 = (bf16[80,4096]{1,0:T(8,128)(2,1)S(1)}, bf16[80,4096]{1,0:T(8,128)(2,1)S(1)}, u32[]{:S(2)}, u32[]{:S(2)}) collective-permute-start(bf16[80,4096]{1,0:T(8,128)(2,1)S(1)} %collective-permute-done.4), channel_id=1, source_target_pairs={{0,32},{1,481},{2,34},{3,483},{4,36},{5,485},{6,38},{7,487},{8,40}... | collective-permute-start | bytes 1966088 | tf_op jit(solution)/shard_map/ppermute | solution.py:41
  54.3 2.6 %collective-permute-start.9 = (bf16[80,4096]{1,0:T(8,128)(2,1)S(1)}, bf16[80,4096]{1,0:T(8,128)(2,1)S(1)}, u32[]{:S(2)}, u32[]{:S(2)}) collective-permute-start(bf16[80,4096]{1,0:T(8,128)(2,1)S(1)} %collective-permute-done.7), channel_id=1, source_target_pairs={{0,32},{1,481},{2,34},{3,483},{4,36},{5,485},{6,38},{7,487},{8,40}... | collective-permute-start | bytes 1966088 | tf_op jit(solution)/shard_map/ppermute | solution.py:41
  57.4 1.8 %collective-permute-done.6 = bf16[80,4096]{1,0:T(8,128)(2,1)S(1)} collective-permute-done((bf16[80,4096]{1,0:T(8,128)(2,1)S(1)}, bf16[80,4096]{1,0:T(8,128)(2,1)S(1)}, u32[]{:S(2)}, u32[]{:S(2)}) %collective-permute-start.6) | collective-permute-done | bytes 655392 | tf_op jit(solution)/shard_map/ppermute | solution.py:41
  59.2 5.0 %collective-permute-start.8 = (bf16[80,4096]{1,0:T(8,128)(2,1)S(1)}, bf16[80,4096]{1,0:T(8,128)(2,1)S(1)}, u32[]{:S(2)}, u32[]{:S(2)}) collective-permute-start(bf16[80,4096]{1,0:T(8,128)(2,1)S(1)} %collective-permute-done.6), channel_id=1, source_target_pairs={{0,32},{1,481},{2,34},{3,483},{4,36},{5,485},{6,38},{7,487},{8,40}... | collective-permute-start | bytes 1966088 | tf_op jit(solution)/shard_map/ppermute | solution.py:41
  64.2 2.2 %fusion.23 = bf16[16,80,160]{1,2,0:T(8,128)(2,1)} fusion(bf16[16,80,160]{1,2,0:T(8,128)(2,1)} %fusion.25, s32[]{:T(128)S(6)} %select_n.133, f32[160,80]{1,0:T(8,128)S(1)} %fusion.37, bf16[80,4096]{1,0:T(8,128)(2,1)} %collective-permute-done.2, bf16[80,4096]{1,0:T(8,128)(2,1)S(1)} %collective-permute-done, bf16[80,4096]{1,0:T(8,128)(2,1)S(1)} %get-tuple-element.5, ...), kind=kOutput, calls=%fused_computation.35 | convolution fusion | flops 110781440 | bytes 2058245 | tf_op jit(solution)/shard_map/dot_general | solution.py:12
  67.0 4.3 %collective-permute-start.11 = (bf16[80,4096]{1,0:T(8,128)(2,1)S(1)}, bf16[80,4096]{1,0:T(8,128)(2,1)S(1)}, u32[]{:S(2)}, u32[]{:S(2)}) collective-permute-start(bf16[80,4096]{1,0:T(8,128)(2,1)S(1)} %collective-permute-done.9), channel_id=1, source_target_pairs={{0,32},{1,481},{2,34},{3,483},{4,36},{5,485},{6,38},{7,487},{8,40}... | collective-permute-start | bytes 1966088 | tf_op jit(solution)/shard_map/ppermute | solution.py:41
  73.3 5.0 %collective-permute-start.10 = (bf16[80,4096]{1,0:T(8,128)(2,1)S(1)}, bf16[80,4096]{1,0:T(8,128)(2,1)S(1)}, u32[]{:S(2)}, u32[]{:S(2)}) collective-permute-start(bf16[80,4096]{1,0:T(8,128)(2,1)S(1)} %collective-permute-done.8), channel_id=1, source_target_pairs={{0,32},{1,481},{2,34},{3,483},{4,36},{5,485},{6,38},{7,487},{8,40}... | collective-permute-start | bytes 1966088 | tf_op jit(solution)/shard_map/ppermute | solution.py:41
  80.3 5.0 %collective-permute-start.13 = (bf16[80,4096]{1,0:T(8,128)(2,1)S(1)}, bf16[80,4096]{1,0:T(8,128)(2,1)S(1)}, u32[]{:S(2)}, u32[]{:S(2)}) collective-permute-start(bf16[80,4096]{1,0:T(8,128)(2,1)S(1)} %collective-permute-done.11), channel_id=1, source_target_pairs={{0,32},{1,481},{2,34},{3,483},{4,36},{5,485},{6,38},{7,487},{8,40}... | collective-permute-start | bytes 1966088 | tf_op jit(solution)/shard_map/ppermute | solution.py:41
  85.8 1.5 collective-permute-done.10
  87.3 5.0 %collective-permute-start.12 = (bf16[80,4096]{1,0:T(8,128)(2,1)S(1)}, bf16[80,4096]{1,0:T(8,128)(2,1)S(1)}, u32[]{:S(2)}, u32[]{:S(2)}) collective-permute-start(bf16[80,4096]{1,0:T(8,128)(2,1)S(1)} %collective-permute-done.10), channel_id=1, source_target_pairs={{0,32},{1,481},{2,34},{3,483},{4,36},{5,485},{6,38},{7,487},{8,40}... | collective-permute-start | bytes 1966088 | tf_op jit(solution)/shard_map/ppermute | solution.py:41
  94.3 5.0 %collective-permute-start.15 = (bf16[80,4096]{1,0:T(8,128)(2,1)S(1)}, bf16[80,4096]{1,0:T(8,128)(2,1)S(1)}, u32[]{:S(2)}, u32[]{:S(2)}) collective-permute-start(bf16[80,4096]{1,0:T(8,128)(2,1)S(1)} %collective-permute-done.13), channel_id=1, source_target_pairs={{0,32},{1,481},{2,34},{3,483},{4,36},{5,485},{6,38},{7,487},{8,40}... | collective-permute-start | bytes 1966088 | tf_op jit(solution)/shard_map/ppermute | solution.py:41
  101.4 5.0 %collective-permute-start.14 = (bf16[80,4096]{1,0:T(8,128)(2,1)S(1)}, bf16[80,4096]{1,0:T(8,128)(2,1)S(1)}, u32[]{:S(2)}, u32[]{:S(2)}) collective-permute-start(bf16[80,4096]{1,0:T(8,128)(2,1)S(1)} %collective-permute-done.12), channel_id=1, source_target_pairs={{0,32},{1,481},{2,34},{3,483},{4,36},{5,485},{6,38},{7,487},{8,40}... | collective-permute-start | bytes 1966088 | tf_op jit(solution)/shard_map/ppermute | solution.py:41
  108.4 5.0 %collective-permute-start.17 = (bf16[80,2048]{1,0:T(8,128)(2,1)S(1)}, bf16[80,2048]{1,0:T(8,128)(2,1)S(1)}, u32[]{:S(2)}, u32[]{:S(2)}) collective-permute-start(bf16[80,2048]{1,0:T(8,128)(2,1)S(1)} %constant_dynamic-slice_fusion.2), channel_id=1, source_target_pairs={{0,32},{1,481},{2,34},{3,483},{4,36},{5,485},{6,38},{7,487},{8,40}... | collective-permute-start | bytes 983048 | tf_op jit(solution)/shard_map/ppermute | solution.py:41
  113.4 2.0 %collective-permute-done.14 = bf16[80,4096]{1,0:T(8,128)(2,1)S(1)} collective-permute-done((bf16[80,4096]{1,0:T(8,128)(2,1)S(1)}, bf16[80,4096]{1,0:T(8,128)(2,1)S(1)}, u32[]{:S(2)}, u32[]{:S(2)}) %collective-permute-start.14) | collective-permute-done | bytes 655392 | tf_op jit(solution)/shard_map/ppermute | solution.py:41
  115.4 5.0 %collective-permute-start.16 = (bf16[80,2048]{1,0:T(8,128)(2,1)S(1)}, bf16[80,2048]{1,0:T(8,128)(2,1)S(1)}, u32[]{:S(2)}, u32[]{:S(2)}) collective-permute-start(bf16[80,2048]{1,0:T(8,128)(2,1)S(1)} %constant_dynamic-slice_fusion.3), channel_id=1, source_target_pairs={{0,32},{1,481},{2,34},{3,483},{4,36},{5,485},{6,38},{7,487},{8,40}... | collective-permute-start | bytes 983048 | tf_op jit(solution)/shard_map/ppermute | solution.py:41
  122.5 2.0 %collective-permute-done.16 = bf16[80,2048]{1,0:T(8,128)(2,1)S(1)} collective-permute-done((bf16[80,2048]{1,0:T(8,128)(2,1)S(1)}, bf16[80,2048]{1,0:T(8,128)(2,1)S(1)}, u32[]{:S(2)}, u32[]{:S(2)}) %collective-permute-start.16) | collective-permute-done | bytes 327712 | tf_op jit(solution)/shard_map/ppermute | solution.py:41
  125.5 8.1 %all-to-all-start = ((bf16[16,80,160]{1,2,0:T(8,128)(2,1)}), bf16[16,80,160]{1,2,0:T(8,128)(2,1)S(1)}, u32[]{:S(2)}, u32[]{:S(2)}) async-start(bf16[16,80,160]{1,2,0:T(8,128)(2,1)} %constant_dynamic-update-slice_fusion), calls=%async_computation | async-start | bytes 1310720 | tf_op jit(solution)/shard_map/all_to_all | solution.py:68
  133.7 8.9 %all-to-all-done = bf16[16,80,160]{1,2,0:T(8,128)(2,1)S(1)} async-done(((bf16[16,80,160]{1,2,0:T(8,128)(2,1)}), bf16[16,80,160]{1,2,0:T(8,128)(2,1)S(1)}, u32[]{:S(2)}, u32[]{:S(2)}) %all-to-all-start) | async-done | bytes 409632 | tf_op jit(solution)/shard_map/all_to_all | solution.py:68
  142.7 5.6 %collective-permute-start.19 = (f32[80,160]{0,1:T(8,128)S(1)}, f32[80,160]{0,1:T(8,128)S(1)}, u32[]{:S(2)}, u32[]{:S(2)}) collective-permute-start(f32[80,160]{0,1:T(8,128)S(1)} %convert_reduce_fusion), channel_id=1, source_target_pairs={{1,32},{2,64},{3,96},{4,128},{5,160},{6,192},{7,224},{8,256},{9,28... | collective-permute-start | bytes 153608 | tf_op jit(solution)/shard_map/ppermute | solution.py:77
  148.4 3.0 %collective-permute-start.18 = (f32[80,80]{1,0:T(8,128)S(1)}, f32[80,80]{1,0:T(8,128)S(1)}, u32[]{:S(2)}, u32[]{:S(2)}) collective-permute-start(f32[80,80]{1,0:T(8,128)S(1)} %copy.9), channel_id=1, source_target_pairs={{0,16},{16,0},{32,48},{48,32},{64,80},{80,64},{96,112},{112,96},{1... | collective-permute-start | bytes 76808 | tf_op jit(solution)/shard_map/ppermute | solution.py:80
  151.5 3.4 %collective-permute-done.18 = f32[80,80]{1,0:T(8,128)S(1)} collective-permute-done((f32[80,80]{1,0:T(8,128)S(1)}, f32[80,80]{1,0:T(8,128)S(1)}, u32[]{:S(2)}, u32[]{:S(2)}) %collective-permute-start.18) | collective-permute-done | bytes 25632 | tf_op jit(solution)/shard_map/ppermute | solution.py:80
  155.0 7.1 %collective-permute-done.19 = f32[80,160]{0,1:T(8,128)S(1)} collective-permute-done((f32[80,160]{0,1:T(8,128)S(1)}, f32[80,160]{0,1:T(8,128)S(1)}, u32[]{:S(2)}, u32[]{:S(2)}) %collective-permute-start.19) | collective-permute-done | bytes 51232 | tf_op jit(solution)/shard_map/ppermute | solution.py:77
  (44 shorter events, 20.0 us)
Async XLA Ops:
  1.4 18.6 %collective-permute-start.3 = (bf16[80,4096]{1,0:T(8,128)(2,1)S(1)}, bf16[80,4096]{1,0:T(8,128)(2,1)S(1)}, u32[]{:S(2)}, u32[]{:S(2)}) collective-permute-start(bf16[80,4096]{1,0:T(8,128)(2,1)S(1)} %get-tuple-element.6), channel_id=1, source_target_pairs={{0,32},{1,481},{2,34},{3,483},{4,36},{5,485},{6,38},{7,487},{8,40}... | collective-permute-start | bytes 1966088 | tf_op jit(solution)/shard_map/ppermute | solution.py:41
  12.5 16.1 %collective-permute-start.2 = (bf16[80,4096]{1,0:T(8,128)(2,1)S(1)}, bf16[80,4096]{1,0:T(8,128)(2,1)}, u32[]{:S(2)}, u32[]{:S(2)}) collective-permute-start(bf16[80,4096]{1,0:T(8,128)(2,1)S(1)} %get-tuple-element.5), channel_id=1, source_target_pairs={{0,32},{1,481},{2,34},{3,483},{4,36},{5,485},{6,38},{7,487},{8,40}... | collective-permute-start | bytes 1966088 | tf_op jit(solution)/shard_map/ppermute | solution.py:41
  15.2 17.3 %collective-permute-start.1 = (bf16[80,4096]{1,0:T(8,128)(2,1)S(1)}, bf16[80,4096]{1,0:T(8,128)(2,1)}, u32[]{:S(2)}, u32[]{:S(2)}) collective-permute-start(bf16[80,4096]{1,0:T(8,128)(2,1)S(1)} %get-tuple-element.6), channel_id=1, source_target_pairs={{0,16},{16,0},{32,48},{48,32},{64,80},{80,64},{96,112},{112,96},{1... | collective-permute-start | bytes 1966088 | tf_op jit(solution)/shard_map/ppermute | solution.py:52
  20.0 14.1 %collective-permute-start.5 = (bf16[80,4096]{1,0:T(8,128)(2,1)S(1)}, bf16[80,4096]{1,0:T(8,128)(2,1)S(1)}, u32[]{:S(2)}, u32[]{:S(2)}) collective-permute-start(bf16[80,4096]{1,0:T(8,128)(2,1)S(1)} %collective-permute-done.3), channel_id=1, source_target_pairs={{0,32},{1,481},{2,34},{3,483},{4,36},{5,485},{6,38},{7,487},{8,40}... | collective-permute-start | bytes 1966088 | tf_op jit(solution)/shard_map/ppermute | solution.py:41
  25.5 18.8 %collective-permute-start = (bf16[80,4096]{1,0:T(8,128)(2,1)S(1)}, bf16[80,4096]{1,0:T(8,128)(2,1)S(1)}, u32[]{:S(2)}, u32[]{:S(2)}) collective-permute-start(bf16[80,4096]{1,0:T(8,128)(2,1)S(1)} %get-tuple-element.5), channel_id=1, source_target_pairs={{0,16},{16,0},{32,48},{48,32},{64,80},{80,64},{96,112},{112,96},{1... | collective-permute-start | bytes 1966088 | tf_op jit(solution)/shard_map/ppermute | solution.py:52
  28.6 15.9 %collective-permute-start.4 = (bf16[80,4096]{1,0:T(8,128)(2,1)}, bf16[80,4096]{1,0:T(8,128)(2,1)S(1)}, u32[]{:S(2)}, u32[]{:S(2)}) collective-permute-start(bf16[80,4096]{1,0:T(8,128)(2,1)} %collective-permute-done.2), channel_id=1, source_target_pairs={{0,32},{1,481},{2,34},{3,483},{4,36},{5,485},{6,38},{7,487},{8,40}... | collective-permute-start | bytes 1966088 | tf_op jit(solution)/shard_map/ppermute | solution.py:41
  34.1 17.6 %copy-start = (bf16[80,8192]{1,0:T(8,128)(2,1)S(1)}, bf16[80,8192]{1,0:T(8,128)(2,1)}, u32[]{:S(2)}) copy-start(bf16[80,8192]{1,0:T(8,128)(2,1)} %param.1) | copy-start | bytes 3932164
  34.1 20.2 %collective-permute-start.7 = (bf16[80,4096]{1,0:T(8,128)(2,1)S(1)}, bf16[80,4096]{1,0:T(8,128)(2,1)S(1)}, u32[]{:S(2)}, u32[]{:S(2)}) collective-permute-start(bf16[80,4096]{1,0:T(8,128)(2,1)S(1)} %collective-permute-done.5), channel_id=1, source_target_pairs={{0,32},{1,481},{2,34},{3,483},{4,36},{5,485},{6,38},{7,487},{8,40}... | collective-permute-start | bytes 1966088 | tf_op jit(solution)/shard_map/ppermute | solution.py:41
  44.6 14.7 %collective-permute-start.6 = (bf16[80,4096]{1,0:T(8,128)(2,1)S(1)}, bf16[80,4096]{1,0:T(8,128)(2,1)S(1)}, u32[]{:S(2)}, u32[]{:S(2)}) collective-permute-start(bf16[80,4096]{1,0:T(8,128)(2,1)S(1)} %collective-permute-done.4), channel_id=1, source_target_pairs={{0,32},{1,481},{2,34},{3,483},{4,36},{5,485},{6,38},{7,487},{8,40}... | collective-permute-start | bytes 1966088 | tf_op jit(solution)/shard_map/ppermute | solution.py:41
  54.3 12.7 %collective-permute-start.9 = (bf16[80,4096]{1,0:T(8,128)(2,1)S(1)}, bf16[80,4096]{1,0:T(8,128)(2,1)S(1)}, u32[]{:S(2)}, u32[]{:S(2)}) collective-permute-start(bf16[80,4096]{1,0:T(8,128)(2,1)S(1)} %collective-permute-done.7), channel_id=1, source_target_pairs={{0,32},{1,481},{2,34},{3,483},{4,36},{5,485},{6,38},{7,487},{8,40}... | collective-permute-start | bytes 1966088 | tf_op jit(solution)/shard_map/ppermute | solution.py:41
  59.2 14.0 %collective-permute-start.8 = (bf16[80,4096]{1,0:T(8,128)(2,1)S(1)}, bf16[80,4096]{1,0:T(8,128)(2,1)S(1)}, u32[]{:S(2)}, u32[]{:S(2)}) collective-permute-start(bf16[80,4096]{1,0:T(8,128)(2,1)S(1)} %collective-permute-done.6), channel_id=1, source_target_pairs={{0,32},{1,481},{2,34},{3,483},{4,36},{5,485},{6,38},{7,487},{8,40}... | collective-permute-start | bytes 1966088 | tf_op jit(solution)/shard_map/ppermute | solution.py:41
  67.0 13.3 %collective-permute-start.11 = (bf16[80,4096]{1,0:T(8,128)(2,1)S(1)}, bf16[80,4096]{1,0:T(8,128)(2,1)S(1)}, u32[]{:S(2)}, u32[]{:S(2)}) collective-permute-start(bf16[80,4096]{1,0:T(8,128)(2,1)S(1)} %collective-permute-done.9), channel_id=1, source_target_pairs={{0,32},{1,481},{2,34},{3,483},{4,36},{5,485},{6,38},{7,487},{8,40}... | collective-permute-start | bytes 1966088 | tf_op jit(solution)/shard_map/ppermute | solution.py:41
  73.3 14.0 %collective-permute-start.10 = (bf16[80,4096]{1,0:T(8,128)(2,1)S(1)}, bf16[80,4096]{1,0:T(8,128)(2,1)S(1)}, u32[]{:S(2)}, u32[]{:S(2)}) collective-permute-start(bf16[80,4096]{1,0:T(8,128)(2,1)S(1)} %collective-permute-done.8), channel_id=1, source_target_pairs={{0,32},{1,481},{2,34},{3,483},{4,36},{5,485},{6,38},{7,487},{8,40}... | collective-permute-start | bytes 1966088 | tf_op jit(solution)/shard_map/ppermute | solution.py:41
  80.3 14.0 %collective-permute-start.13 = (bf16[80,4096]{1,0:T(8,128)(2,1)S(1)}, bf16[80,4096]{1,0:T(8,128)(2,1)S(1)}, u32[]{:S(2)}, u32[]{:S(2)}) collective-permute-start(bf16[80,4096]{1,0:T(8,128)(2,1)S(1)} %collective-permute-done.11), channel_id=1, source_target_pairs={{0,32},{1,481},{2,34},{3,483},{4,36},{5,485},{6,38},{7,487},{8,40}... | collective-permute-start | bytes 1966088 | tf_op jit(solution)/shard_map/ppermute | solution.py:41
  87.3 14.0 %collective-permute-start.12 = (bf16[80,4096]{1,0:T(8,128)(2,1)S(1)}, bf16[80,4096]{1,0:T(8,128)(2,1)S(1)}, u32[]{:S(2)}, u32[]{:S(2)}) collective-permute-start(bf16[80,4096]{1,0:T(8,128)(2,1)S(1)} %collective-permute-done.10), channel_id=1, source_target_pairs={{0,32},{1,481},{2,34},{3,483},{4,36},{5,485},{6,38},{7,487},{8,40}... | collective-permute-start | bytes 1966088 | tf_op jit(solution)/shard_map/ppermute | solution.py:41
  94.3 14.0 %collective-permute-start.15 = (bf16[80,4096]{1,0:T(8,128)(2,1)S(1)}, bf16[80,4096]{1,0:T(8,128)(2,1)S(1)}, u32[]{:S(2)}, u32[]{:S(2)}) collective-permute-start(bf16[80,4096]{1,0:T(8,128)(2,1)S(1)} %collective-permute-done.13), channel_id=1, source_target_pairs={{0,32},{1,481},{2,34},{3,483},{4,36},{5,485},{6,38},{7,487},{8,40}... | collective-permute-start | bytes 1966088 | tf_op jit(solution)/shard_map/ppermute | solution.py:41
  101.4 14.0 %collective-permute-start.14 = (bf16[80,4096]{1,0:T(8,128)(2,1)S(1)}, bf16[80,4096]{1,0:T(8,128)(2,1)S(1)}, u32[]{:S(2)}, u32[]{:S(2)}) collective-permute-start(bf16[80,4096]{1,0:T(8,128)(2,1)S(1)} %collective-permute-done.12), channel_id=1, source_target_pairs={{0,32},{1,481},{2,34},{3,483},{4,36},{5,485},{6,38},{7,487},{8,40}... | collective-permute-start | bytes 1966088 | tf_op jit(solution)/shard_map/ppermute | solution.py:41
  108.4 13.7 %collective-permute-start.17 = (bf16[80,2048]{1,0:T(8,128)(2,1)S(1)}, bf16[80,2048]{1,0:T(8,128)(2,1)S(1)}, u32[]{:S(2)}, u32[]{:S(2)}) collective-permute-start(bf16[80,2048]{1,0:T(8,128)(2,1)S(1)} %constant_dynamic-slice_fusion.2), channel_id=1, source_target_pairs={{0,32},{1,481},{2,34},{3,483},{4,36},{5,485},{6,38},{7,487},{8,40}... | collective-permute-start | bytes 983048 | tf_op jit(solution)/shard_map/ppermute | solution.py:41
  115.4 9.0 %collective-permute-start.16 = (bf16[80,2048]{1,0:T(8,128)(2,1)S(1)}, bf16[80,2048]{1,0:T(8,128)(2,1)S(1)}, u32[]{:S(2)}, u32[]{:S(2)}) collective-permute-start(bf16[80,2048]{1,0:T(8,128)(2,1)S(1)} %constant_dynamic-slice_fusion.3), channel_id=1, source_target_pairs={{0,32},{1,481},{2,34},{3,483},{4,36},{5,485},{6,38},{7,487},{8,40}... | collective-permute-start | bytes 983048 | tf_op jit(solution)/shard_map/ppermute | solution.py:41
  125.5 17.0 %all-to-all-start = ((bf16[16,80,160]{1,2,0:T(8,128)(2,1)}), bf16[16,80,160]{1,2,0:T(8,128)(2,1)S(1)}, u32[]{:S(2)}, u32[]{:S(2)}) async-start(bf16[16,80,160]{1,2,0:T(8,128)(2,1)} %constant_dynamic-update-slice_fusion), calls=%async_computation | async-start | bytes 1310720 | tf_op jit(solution)/shard_map/all_to_all | solution.py:68
  142.7 19.4 %collective-permute-start.19 = (f32[80,160]{0,1:T(8,128)S(1)}, f32[80,160]{0,1:T(8,128)S(1)}, u32[]{:S(2)}, u32[]{:S(2)}) collective-permute-start(f32[80,160]{0,1:T(8,128)S(1)} %convert_reduce_fusion), channel_id=1, source_target_pairs={{1,32},{2,64},{3,96},{4,128},{5,160},{6,192},{7,224},{8,256},{9,28... | collective-permute-start | bytes 153608 | tf_op jit(solution)/shard_map/ppermute | solution.py:77
  148.4 6.5 %collective-permute-start.18 = (f32[80,80]{1,0:T(8,128)S(1)}, f32[80,80]{1,0:T(8,128)S(1)}, u32[]{:S(2)}, u32[]{:S(2)}) collective-permute-start(f32[80,80]{1,0:T(8,128)S(1)} %copy.9), channel_id=1, source_target_pairs={{0,16},{16,0},{32,48},{48,32},{64,80},{80,64},{96,112},{112,96},{1... | collective-permute-start | bytes 76808 | tf_op jit(solution)/shard_map/ppermute | solution.py:80

commit v4 on v2

--- a/solution.py
+++ b/solution.py
@@ -42,10 +42,13 @@
 
     strip = jnp.zeros((planes, rows, 2 * rows), jnp.bfloat16)
 
+    def slot_of(place):
+        return place % 2 * (par_size // 2) + place // 2
+
     def put(strip, travel, held, where):
         tile = sum(tile_of(block, block_held) for block, block_held in zip(travel, held))
         return lax.dynamic_update_slice_in_dim(
-            strip, tile.astype(jnp.bfloat16)[None], jnp.mod(where, planes), 0
+            strip, tile.astype(jnp.bfloat16)[None], slot_of(jnp.mod(where, planes)), 0
         )
 
     mine = [lax.slice_in_dim(jacobian, c * width, (c + 1) * width, axis=1) for c in range(CHUNKS)]
@@ -64,7 +67,8 @@
     held = [side_of(block, plane // half) for block in own]
     strip = put(strip, travel, held, plane + half)
 
-    groups = [[e * par_size + p for p in range(par_size)] for e in range(ex_size)]
+    by_slot = sorted(range(par_size), key=slot_of)
+    groups = [[e * par_size + p for p in by_slot] for e in range(ex_size)]
     parts = lax.all_to_all(strip, AXES, 0, 0, axis_index_groups=groups, tiled=True)
     total = jnp.sum(parts.astype(jnp.float32), axis=0)
     mirror = [

time: 163 us -> 162 us (level)
  transfers between devices with their start and end apart: 21 -> 21, of which waited for: 17 -> 16; matrix products, arithmetic and copies ran while one was open for 11% -> 11% of each run, Pallas kernels for 0% -> 0%
where the time goes in v4:
time: 162 us
  waiting for transfers between devices  75.3 us (46%)
  starting transfers between devices  64.3 us (40%)
  matrix products  15.1 us (9%)
  local copies, waits for them, and re-layouts  3.39 us (2%)
  other arithmetic  2.73 us (2%)
    ppermute x16, waiting for transfers between devices, hop(): return lax.ppermute(block, AXES, onward)  56.6 us
    ppermute x16, starting transfers between devices, hop(): return lax.ppermute(block, AXES, onward)  34.4 us
    dot_general x18, matrix products, tile_of(): lax.dot_general(rows_a, rows_b, (((1,), (1,)), ((), ())), preferred_eleme...  15.1 us
    ppermute x2, starting transfers between devices, shards(): own = [in_order(block, lax.ppermute(block, 'ex', swap)) for block in mine]  9.87 us
    all_to_all x1, waiting for transfers between devices, shards(): lax.all_to_all(strip, AXES, 0, 0, axis_index_groups=groups, tiled=True)  9.86 us
    ppermute x1, starting transfers between devices, shards(): added = lax.ppermute(packed, AXES, mirror).reshape(rows, 2 * rows)  9.62 us
    ppermute x2, waiting for transfers between devices, shards(): own = [in_order(block, lax.ppermute(block, 'ex', swap)) for block in mine]  5.91 us
    all_to_all x1, starting transfers between devices, shards(): lax.all_to_all(strip, AXES, 0, 0, axis_index_groups=groups, tiled=True)  5.75 us
  transfers between devices with their start and end apart: 21, of which 16 were waited for; matrix products, arithmetic and copies ran while one was open for 11% of the time, Pallas kernels for 0%

profile of v4, /device:TPU:16, one launch (start us, length us, event | category | flops | bytes accessed | tf_op | source)
XLA Modules:
  0.0 161.7 jit_solution(5755174620692710411)
XLA Ops:
  1.4 3.8 %collective-permute-start.3 = (bf16[80,4096]{1,0:T(8,128)(2,1)S(1)}, bf16[80,4096]{1,0:T(8,128)(2,1)S(1)}, u32[]{:S(2)}, u32[]{:S(2)}) collective-permute-start(bf16[80,4096]{1,0:T(8,128)(2,1)S(1)} %get-tuple-element.6), channel_id=1, source_target_pairs={{0,32},{1,481},{2,34},{3,483},{4,36},{5,485},{6,38},{7,487},{8,40}... | collective-permute-start | bytes 1966088 | tf_op jit(solution)/shard_map/ppermute | solution.py:41
  5.2 3.8 %collective-permute-start.2 = (bf16[80,4096]{1,0:T(8,128)(2,1)S(1)}, bf16[80,4096]{1,0:T(8,128)(2,1)}, u32[]{:S(2)}, u32[]{:S(2)}) collective-permute-start(bf16[80,4096]{1,0:T(8,128)(2,1)S(1)} %get-tuple-element.5), channel_id=1, source_target_pairs={{0,32},{1,481},{2,34},{3,483},{4,36},{5,485},{6,38},{7,487},{8,40}... | collective-permute-start | bytes 1966088 | tf_op jit(solution)/shard_map/ppermute | solution.py:41
  9.1 4.9 %collective-permute-start.1 = (bf16[80,4096]{1,0:T(8,128)(2,1)S(1)}, bf16[80,4096]{1,0:T(8,128)(2,1)}, u32[]{:S(2)}, u32[]{:S(2)}) collective-permute-start(bf16[80,4096]{1,0:T(8,128)(2,1)S(1)} %get-tuple-element.6), channel_id=1, source_target_pairs={{0,16},{16,0},{32,48},{48,32},{64,80},{80,64},{96,112},{112,96},{1... | collective-permute-start | bytes 1966088 | tf_op jit(solution)/shard_map/ppermute | solution.py:55
  14.0 7.4 %collective-permute-done.3 = bf16[80,4096]{1,0:T(8,128)(2,1)S(1)} collective-permute-done((bf16[80,4096]{1,0:T(8,128)(2,1)S(1)}, bf16[80,4096]{1,0:T(8,128)(2,1)S(1)}, u32[]{:S(2)}, u32[]{:S(2)}) %collective-permute-start.3) | collective-permute-done | bytes 655392 | tf_op jit(solution)/shard_map/ppermute | solution.py:41
  21.4 1.9 %collective-permute-start.5 = (bf16[80,4096]{1,0:T(8,128)(2,1)S(1)}, bf16[80,4096]{1,0:T(8,128)(2,1)S(1)}, u32[]{:S(2)}, u32[]{:S(2)}) collective-permute-start(bf16[80,4096]{1,0:T(8,128)(2,1)S(1)} %collective-permute-done.3), channel_id=1, source_target_pairs={{0,32},{1,481},{2,34},{3,483},{4,36},{5,485},{6,38},{7,487},{8,40}... | collective-permute-start | bytes 1966088 | tf_op jit(solution)/shard_map/ppermute | solution.py:41
  23.3 4.9 %collective-permute-start = (bf16[80,4096]{1,0:T(8,128)(2,1)S(1)}, bf16[80,4096]{1,0:T(8,128)(2,1)S(1)}, u32[]{:S(2)}, u32[]{:S(2)}) collective-permute-start(bf16[80,4096]{1,0:T(8,128)(2,1)S(1)} %get-tuple-element.5), channel_id=1, source_target_pairs={{0,16},{16,0},{32,48},{48,32},{64,80},{80,64},{96,112},{112,96},{1... | collective-permute-start | bytes 1966088 | tf_op jit(solution)/shard_map/ppermute | solution.py:55
  28.8 1.9 %collective-permute-start.4 = (bf16[80,4096]{1,0:T(8,128)(2,1)}, bf16[80,4096]{1,0:T(8,128)(2,1)S(1)}, u32[]{:S(2)}, u32[]{:S(2)}) collective-permute-start(bf16[80,4096]{1,0:T(8,128)(2,1)} %collective-permute-done.2), channel_id=1, source_target_pairs={{0,32},{1,481},{2,34},{3,483},{4,36},{5,485},{6,38},{7,487},{8,40}... | collective-permute-start | bytes 1966088 | tf_op jit(solution)/shard_map/ppermute | solution.py:41
  32.3 3.1 %collective-permute-done.5 = bf16[80,4096]{1,0:T(8,128)(2,1)S(1)} collective-permute-done((bf16[80,4096]{1,0:T(8,128)(2,1)S(1)}, bf16[80,4096]{1,0:T(8,128)(2,1)S(1)}, u32[]{:S(2)}, u32[]{:S(2)}) %collective-permute-start.5) | collective-permute-done | bytes 655392 | tf_op jit(solution)/shard_map/ppermute | solution.py:41
  35.4 1.9 %collective-permute-start.7 = (bf16[80,4096]{1,0:T(8,128)(2,1)S(1)}, bf16[80,4096]{1,0:T(8,128)(2,1)S(1)}, u32[]{:S(2)}, u32[]{:S(2)}) collective-permute-start(bf16[80,4096]{1,0:T(8,128)(2,1)S(1)} %collective-permute-done.5), channel_id=1, source_target_pairs={{0,32},{1,481},{2,34},{3,483},{4,36},{5,485},{6,38},{7,487},{8,40}... | collective-permute-start | bytes 1966088 | tf_op jit(solution)/shard_map/ppermute | solution.py:41
  37.3 5.9 %collective-permute-done = bf16[80,4096]{1,0:T(8,128)(2,1)S(1)} collective-permute-done((bf16[80,4096]{1,0:T(8,128)(2,1)S(1)}, bf16[80,4096]{1,0:T(8,128)(2,1)S(1)}, u32[]{:S(2)}, u32[]{:S(2)}) %collective-permute-start) | collective-permute-done | bytes 655392 | tf_op jit(solution)/shard_map/ppermute | solution.py:55
  43.5 1.9 %collective-permute-start.6 = (bf16[80,4096]{1,0:T(8,128)(2,1)S(1)}, bf16[80,4096]{1,0:T(8,128)(2,1)S(1)}, u32[]{:S(2)}, u32[]{:S(2)}) collective-permute-start(bf16[80,4096]{1,0:T(8,128)(2,1)S(1)} %collective-permute-done.4), channel_id=1, source_target_pairs={{0,32},{1,481},{2,34},{3,483},{4,36},{5,485},{6,38},{7,487},{8,40}... | collective-permute-start | bytes 1966088 | tf_op jit(solution)/shard_map/ppermute | solution.py:41
  49.7 1.9 %collective-permute-start.9 = (bf16[80,4096]{1,0:T(8,128)(2,1)S(1)}, bf16[80,4096]{1,0:T(8,128)(2,1)S(1)}, u32[]{:S(2)}, u32[]{:S(2)}) collective-permute-start(bf16[80,4096]{1,0:T(8,128)(2,1)S(1)} %collective-permute-done.7), channel_id=1, source_target_pairs={{0,32},{1,481},{2,34},{3,483},{4,36},{5,485},{6,38},{7,487},{8,40}... | collective-permute-start | bytes 1966088 | tf_op jit(solution)/shard_map/ppermute | solution.py:41
  52.1 8.1 %collective-permute-done.6 = bf16[80,4096]{1,0:T(8,128)(2,1)S(1)} collective-permute-done((bf16[80,4096]{1,0:T(8,128)(2,1)S(1)}, bf16[80,4096]{1,0:T(8,128)(2,1)S(1)}, u32[]{:S(2)}, u32[]{:S(2)}) %collective-permute-start.6) | collective-permute-done | bytes 655392 | tf_op jit(solution)/shard_map/ppermute | solution.py:41
  60.3 1.9 %collective-permute-start.8 = (bf16[80,4096]{1,0:T(8,128)(2,1)S(1)}, bf16[80,4096]{1,0:T(8,128)(2,1)S(1)}, u32[]{:S(2)}, u32[]{:S(2)}) collective-permute-start(bf16[80,4096]{1,0:T(8,128)(2,1)S(1)} %collective-permute-done.6), channel_id=1, source_target_pairs={{0,32},{1,481},{2,34},{3,483},{4,36},{5,485},{6,38},{7,487},{8,40}... | collective-permute-start | bytes 1966088 | tf_op jit(solution)/shard_map/ppermute | solution.py:41
  62.2 2.2 %fusion.23 = bf16[16,80,160]{1,2,0:T(8,128)(2,1)} fusion(bf16[16,80,160]{1,2,0:T(8,128)(2,1)} %fusion.25, s32[]{:T(128)S(6)} %select_n.200, f32[160,80]{1,0:T(8,128)S(1)} %fusion.37, bf16[80,4096]{1,0:T(8,128)(2,1)} %collective-permute-done.2, bf16[80,4096]{1,0:T(8,128)(2,1)S(1)} %collective-permute-done, bf16[80,4096]{1,0:T(8,128)(2,1)S(1)} %get-tuple-element.5, ...), kind=kOutput, calls=%fused_computation.35 | convolution fusion | flops 110781440 | bytes 2058245 | tf_op jit(solution)/shard_map/dot_general | solution.py:12
  64.9 2.4 %collective-permute-done.9 = bf16[80,4096]{1,0:T(8,128)(2,1)S(1)} collective-permute-done((bf16[80,4096]{1,0:T(8,128)(2,1)S(1)}, bf16[80,4096]{1,0:T(8,128)(2,1)S(1)}, u32[]{:S(2)}, u32[]{:S(2)}) %collective-permute-start.9) | collective-permute-done | bytes 655392 | tf_op jit(solution)/shard_map/ppermute | solution.py:41
  70.3 4.0 %collective-permute-done.8 = bf16[80,4096]{1,0:T(8,128)(2,1)S(1)} collective-permute-done((bf16[80,4096]{1,0:T(8,128)(2,1)S(1)}, bf16[80,4096]{1,0:T(8,128)(2,1)S(1)}, u32[]{:S(2)}, u32[]{:S(2)}) %collective-permute-start.8) | collective-permute-done | bytes 655392 | tf_op jit(solution)/shard_map/ppermute | solution.py:41
  77.9 3.4 %collective-permute-done.11 = bf16[80,4096]{1,0:T(8,128)(2,1)S(1)} collective-permute-done((bf16[80,4096]{1,0:T(8,128)(2,1)S(1)}, bf16[80,4096]{1,0:T(8,128)(2,1)S(1)}, u32[]{:S(2)}, u32[]{:S(2)}) %collective-permute-start.11) | collective-permute-done | bytes 655392 | tf_op jit(solution)/shard_map/ppermute | solution.py:41
  81.3 1.9 %collective-permute-start.13 = (bf16[80,4096]{1,0:T(8,128)(2,1)S(1)}, bf16[80,4096]{1,0:T(8,128)(2,1)S(1)}, u32[]{:S(2)}, u32[]{:S(2)}) collective-permute-start(bf16[80,4096]{1,0:T(8,128)(2,1)S(1)} %collective-permute-done.11), channel_id=1, source_target_pairs={{0,32},{1,481},{2,34},{3,483},{4,36},{5,485},{6,38},{7,487},{8,40}... | collective-permute-start | bytes 1966088 | tf_op jit(solution)/shard_map/ppermute | solution.py:41
  83.8 4.6 %collective-permute-done.10 = bf16[80,4096]{1,0:T(8,128)(2,1)S(1)} collective-permute-done((bf16[80,4096]{1,0:T(8,128)(2,1)S(1)}, bf16[80,4096]{1,0:T(8,128)(2,1)S(1)}, u32[]{:S(2)}, u32[]{:S(2)}) %collective-permute-start.10) | collective-permute-done | bytes 655392 | tf_op jit(solution)/shard_map/ppermute | solution.py:41
  92.0 3.4 %collective-permute-done.13 = bf16[80,4096]{1,0:T(8,128)(2,1)S(1)} collective-permute-done((bf16[80,4096]{1,0:T(8,128)(2,1)S(1)}, bf16[80,4096]{1,0:T(8,128)(2,1)S(1)}, u32[]{:S(2)}, u32[]{:S(2)}) %collective-permute-start.13) | collective-permute-done | bytes 655392 | tf_op jit(solution)/shard_map/ppermute | solution.py:41
  98.4 4.0 %collective-permute-done.12 = bf16[80,4096]{1,0:T(8,128)(2,1)S(1)} collective-permute-done((bf16[80,4096]{1,0:T(8,128)(2,1)S(1)}, bf16[80,4096]{1,0:T(8,128)(2,1)S(1)}, u32[]{:S(2)}, u32[]{:S(2)}) %collective-permute-start.12) | collective-permute-done | bytes 655392 | tf_op jit(solution)/shard_map/ppermute | solution.py:41
  106.0 3.4 %collective-permute-done.15 = bf16[80,4096]{1,0:T(8,128)(2,1)S(1)} collective-permute-done((bf16[80,4096]{1,0:T(8,128)(2,1)S(1)}, bf16[80,4096]{1,0:T(8,128)(2,1)S(1)}, u32[]{:S(2)}, u32[]{:S(2)}) %collective-permute-start.15) | collective-permute-done | bytes 655392 | tf_op jit(solution)/shard_map/ppermute | solution.py:41
  109.4 1.9 %collective-permute-start.17 = (bf16[80,2048]{1,0:T(8,128)(2,1)S(1)}, bf16[80,2048]{1,0:T(8,128)(2,1)S(1)}, u32[]{:S(2)}, u32[]{:S(2)}) collective-permute-start(bf16[80,2048]{1,0:T(8,128)(2,1)S(1)} %constant_dynamic-slice_fusion.2), channel_id=1, source_target_pairs={{0,32},{1,481},{2,34},{3,483},{4,36},{5,485},{6,38},{7,487},{8,40}... | collective-permute-start | bytes 983048 | tf_op jit(solution)/shard_map/ppermute | solution.py:41
  111.4 5.1 %collective-permute-done.14 = bf16[80,4096]{1,0:T(8,128)(2,1)S(1)} collective-permute-done((bf16[80,4096]{1,0:T(8,128)(2,1)S(1)}, bf16[80,4096]{1,0:T(8,128)(2,1)S(1)}, u32[]{:S(2)}, u32[]{:S(2)}) %collective-permute-start.14) | collective-permute-done | bytes 655392 | tf_op jit(solution)/shard_map/ppermute | solution.py:41
  116.5 1.9 %collective-permute-start.16 = (bf16[80,2048]{1,0:T(8,128)(2,1)S(1)}, bf16[80,2048]{1,0:T(8,128)(2,1)S(1)}, u32[]{:S(2)}, u32[]{:S(2)}) collective-permute-start(bf16[80,2048]{1,0:T(8,128)(2,1)S(1)} %constant_dynamic-slice_fusion.3), channel_id=1, source_target_pairs={{0,32},{1,481},{2,34},{3,483},{4,36},{5,485},{6,38},{7,487},{8,40}... | collective-permute-start | bytes 983048 | tf_op jit(solution)/shard_map/ppermute | solution.py:41
  120.4 6.2 %collective-permute-done.16 = bf16[80,2048]{1,0:T(8,128)(2,1)S(1)} collective-permute-done((bf16[80,2048]{1,0:T(8,128)(2,1)S(1)}, bf16[80,2048]{1,0:T(8,128)(2,1)S(1)}, u32[]{:S(2)}, u32[]{:S(2)}) %collective-permute-start.16) | collective-permute-done | bytes 327712 | tf_op jit(solution)/shard_map/ppermute | solution.py:41
  127.7 5.7 %all-to-all-start = ((bf16[16,80,160]{1,2,0:T(8,128)(2,1)}), bf16[16,80,160]{1,2,0:T(8,128)(2,1)S(1)}, u32[]{:S(2)}, u32[]{:S(2)}) async-start(bf16[16,80,160]{1,2,0:T(8,128)(2,1)} %constant_dynamic-update-slice_fusion), calls=%async_computation | async-start | bytes 1310720 | tf_op jit(solution)/shard_map/all_to_all | solution.py:72
  133.5 9.9 %all-to-all-done = bf16[16,80,160]{1,2,0:T(8,128)(2,1)S(1)} async-done(((bf16[16,80,160]{1,2,0:T(8,128)(2,1)}), bf16[16,80,160]{1,2,0:T(8,128)(2,1)S(1)}, u32[]{:S(2)}, u32[]{:S(2)}) %all-to-all-start) | async-done | bytes 409632 | tf_op jit(solution)/shard_map/all_to_all | solution.py:72
  143.7 9.6 %collective-permute-start.19 = (f32[100,128]{1,0:T(8,128)S(1)}, f32[100,128]{1,0:T(8,128)S(1)}, u32[]{:S(2)}, u32[]{:S(2)}) collective-permute-start(f32[100,128]{1,0:T(8,128)S(1)} %reshape.6), channel_id=1, source_target_pairs={{1,32},{2,64},{3,96},{4,128},{5,160},{6,192},{7,224},{8,256},{9,28... | collective-permute-start | bytes 153608 | tf_op jit(solution)/shard_map/ppermute | solution.py:82
  153.3 4.6 %collective-permute-start.18 = (f32[80,80]{0,1:T(8,128)S(1)}, f32[80,80]{0,1:T(8,128)S(1)}, u32[]{:S(2)}, u32[]{:S(2)}) collective-permute-start(f32[80,80]{0,1:T(8,128)S(1)} %get-tuple-element.8), channel_id=1, source_target_pairs={{0,16},{16,0},{32,48},{48,32},{64,80},{80,64},{96,112},{112,96},{1... | collective-permute-start | bytes 76808 | tf_op jit(solution)/shard_map/ppermute | solution.py:85
  158.0 2.8 %collective-permute-done.19 = f32[100,128]{1,0:T(8,128)S(1)} collective-permute-done((f32[100,128]{1,0:T(8,128)S(1)}, f32[100,128]{1,0:T(8,128)S(1)}, u32[]{:S(2)}, u32[]{:S(2)}) %collective-permute-start.19) | collective-permute-done | bytes 51232 | tf_op jit(solution)/shard_map/ppermute | solution.py:82
  (44 shorter events, 30.2 us)
Async XLA Ops:
  1.4 20.0 %collective-permute-start.3 = (bf16[80,4096]{1,0:T(8,128)(2,1)S(1)}, bf16[80,4096]{1,0:T(8,128)(2,1)S(1)}, u32[]{:S(2)}, u32[]{:S(2)}) collective-permute-start(bf16[80,4096]{1,0:T(8,128)(2,1)S(1)} %get-tuple-element.6), channel_id=1, source_target_pairs={{0,32},{1,481},{2,34},{3,483},{4,36},{5,485},{6,38},{7,487},{8,40}... | collective-permute-start | bytes 1966088 | tf_op jit(solution)/shard_map/ppermute | solution.py:41
  5.2 23.5 %collective-permute-start.2 = (bf16[80,4096]{1,0:T(8,128)(2,1)S(1)}, bf16[80,4096]{1,0:T(8,128)(2,1)}, u32[]{:S(2)}, u32[]{:S(2)}) collective-permute-start(bf16[80,4096]{1,0:T(8,128)(2,1)S(1)} %get-tuple-element.5), channel_id=1, source_target_pairs={{0,32},{1,481},{2,34},{3,483},{4,36},{5,485},{6,38},{7,487},{8,40}... | collective-permute-start | bytes 1966088 | tf_op jit(solution)/shard_map/ppermute | solution.py:41
  9.1 21.6 %collective-permute-start.1 = (bf16[80,4096]{1,0:T(8,128)(2,1)S(1)}, bf16[80,4096]{1,0:T(8,128)(2,1)}, u32[]{:S(2)}, u32[]{:S(2)}) collective-permute-start(bf16[80,4096]{1,0:T(8,128)(2,1)S(1)} %get-tuple-element.6), channel_id=1, source_target_pairs={{0,16},{16,0},{32,48},{48,32},{64,80},{80,64},{96,112},{112,96},{1... | collective-permute-start | bytes 1966088 | tf_op jit(solution)/shard_map/ppermute | solution.py:55
  21.4 14.0 %collective-permute-start.5 = (bf16[80,4096]{1,0:T(8,128)(2,1)S(1)}, bf16[80,4096]{1,0:T(8,128)(2,1)S(1)}, u32[]{:S(2)}, u32[]{:S(2)}) collective-permute-start(bf16[80,4096]{1,0:T(8,128)(2,1)S(1)} %collective-permute-done.3), channel_id=1, source_target_pairs={{0,32},{1,481},{2,34},{3,483},{4,36},{5,485},{6,38},{7,487},{8,40}... | collective-permute-start | bytes 1966088 | tf_op jit(solution)/shard_map/ppermute | solution.py:41
  23.3 20.0 %collective-permute-start = (bf16[80,4096]{1,0:T(8,128)(2,1)S(1)}, bf16[80,4096]{1,0:T(8,128)(2,1)S(1)}, u32[]{:S(2)}, u32[]{:S(2)}) collective-permute-start(bf16[80,4096]{1,0:T(8,128)(2,1)S(1)} %get-tuple-element.5), channel_id=1, source_target_pairs={{0,16},{16,0},{32,48},{48,32},{64,80},{80,64},{96,112},{112,96},{1... | collective-permute-start | bytes 1966088 | tf_op jit(solution)/shard_map/ppermute | solution.py:55
  28.8 14.7 %collective-permute-start.4 = (bf16[80,4096]{1,0:T(8,128)(2,1)}, bf16[80,4096]{1,0:T(8,128)(2,1)S(1)}, u32[]{:S(2)}, u32[]{:S(2)}) collective-permute-start(bf16[80,4096]{1,0:T(8,128)(2,1)} %collective-permute-done.2), channel_id=1, source_target_pairs={{0,32},{1,481},{2,34},{3,483},{4,36},{5,485},{6,38},{7,487},{8,40}... | collective-permute-start | bytes 1966088 | tf_op jit(solution)/shard_map/ppermute | solution.py:41
  32.3 13.2 %copy-start = (bf16[80,8192]{1,0:T(8,128)(2,1)S(1)}, bf16[80,8192]{1,0:T(8,128)(2,1)}, u32[]{:S(2)}) copy-start(bf16[80,8192]{1,0:T(8,128)(2,1)} %param.1) | copy-start | bytes 3932164
  35.4 14.3 %collective-permute-start.7 = (bf16[80,4096]{1,0:T(8,128)(2,1)S(1)}, bf16[80,4096]{1,0:T(8,128)(2,1)S(1)}, u32[]{:S(2)}, u32[]{:S(2)}) collective-permute-start(bf16[80,4096]{1,0:T(8,128)(2,1)S(1)} %collective-permute-done.5), channel_id=1, source_target_pairs={{0,32},{1,481},{2,34},{3,483},{4,36},{5,485},{6,38},{7,487},{8,40}... | collective-permute-start | bytes 1966088 | tf_op jit(solution)/shard_map/ppermute | solution.py:41
  43.5 16.7 %collective-permute-start.6 = (bf16[80,4096]{1,0:T(8,128)(2,1)S(1)}, bf16[80,4096]{1,0:T(8,128)(2,1)S(1)}, u32[]{:S(2)}, u32[]{:S(2)}) collective-permute-start(bf16[80,4096]{1,0:T(8,128)(2,1)S(1)} %collective-permute-done.4), channel_id=1, source_target_pairs={{0,32},{1,481},{2,34},{3,483},{4,36},{5,485},{6,38},{7,487},{8,40}... | collective-permute-start | bytes 1966088 | tf_op jit(solution)/shard_map/ppermute | solution.py:41
  49.7 17.6 %collective-permute-start.9 = (bf16[80,4096]{1,0:T(8,128)(2,1)S(1)}, bf16[80,4096]{1,0:T(8,128)(2,1)S(1)}, u32[]{:S(2)}, u32[]{:S(2)}) collective-permute-start(bf16[80,4096]{1,0:T(8,128)(2,1)S(1)} %collective-permute-done.7), channel_id=1, source_target_pairs={{0,32},{1,481},{2,34},{3,483},{4,36},{5,485},{6,38},{7,487},{8,40}... | collective-permute-start | bytes 1966088 | tf_op jit(solution)/shard_map/ppermute | solution.py:41
  60.3 14.0 %collective-permute-start.8 = (bf16[80,4096]{1,0:T(8,128)(2,1)S(1)}, bf16[80,4096]{1,0:T(8,128)(2,1)S(1)}, u32[]{:S(2)}, u32[]{:S(2)}) collective-permute-start(bf16[80,4096]{1,0:T(8,128)(2,1)S(1)} %collective-permute-done.6), channel_id=1, source_target_pairs={{0,32},{1,481},{2,34},{3,483},{4,36},{5,485},{6,38},{7,487},{8,40}... | collective-permute-start | bytes 1966088 | tf_op jit(solution)/shard_map/ppermute | solution.py:41
  67.3 14.0 %collective-permute-start.11 = (bf16[80,4096]{1,0:T(8,128)(2,1)S(1)}, bf16[80,4096]{1,0:T(8,128)(2,1)S(1)}, u32[]{:S(2)}, u32[]{:S(2)}) collective-permute-start(bf16[80,4096]{1,0:T(8,128)(2,1)S(1)} %collective-permute-done.9), channel_id=1, source_target_pairs={{0,32},{1,481},{2,34},{3,483},{4,36},{5,485},{6,38},{7,487},{8,40}... | collective-permute-start | bytes 1966088 | tf_op jit(solution)/shard_map/ppermute | solution.py:41
  74.3 14.0 %collective-permute-start.10 = (bf16[80,4096]{1,0:T(8,128)(2,1)S(1)}, bf16[80,4096]{1,0:T(8,128)(2,1)S(1)}, u32[]{:S(2)}, u32[]{:S(2)}) collective-permute-start(bf16[80,4096]{1,0:T(8,128)(2,1)S(1)} %collective-permute-done.8), channel_id=1, source_target_pairs={{0,32},{1,481},{2,34},{3,483},{4,36},{5,485},{6,38},{7,487},{8,40}... | collective-permute-start | bytes 1966088 | tf_op jit(solution)/shard_map/ppermute | solution.py:41
  81.3 14.0 %collective-permute-start.13 = (bf16[80,4096]{1,0:T(8,128)(2,1)S(1)}, bf16[80,4096]{1,0:T(8,128)(2,1)S(1)}, u32[]{:S(2)}, u32[]{:S(2)}) collective-permute-start(bf16[80,4096]{1,0:T(8,128)(2,1)S(1)} %collective-permute-done.11), channel_id=1, source_target_pairs={{0,32},{1,481},{2,34},{3,483},{4,36},{5,485},{6,38},{7,487},{8,40}... | collective-permute-start | bytes 1966088 | tf_op jit(solution)/shard_map/ppermute | solution.py:41
  88.3 14.0 %collective-permute-start.12 = (bf16[80,4096]{1,0:T(8,128)(2,1)S(1)}, bf16[80,4096]{1,0:T(8,128)(2,1)S(1)}, u32[]{:S(2)}, u32[]{:S(2)}) collective-permute-start(bf16[80,4096]{1,0:T(8,128)(2,1)S(1)} %collective-permute-done.10), channel_id=1, source_target_pairs={{0,32},{1,481},{2,34},{3,483},{4,36},{5,485},{6,38},{7,487},{8,40}... | collective-permute-start | bytes 1966088 | tf_op jit(solution)/shard_map/ppermute | solution.py:41
  95.4 14.0 %collective-permute-start.15 = (bf16[80,4096]{1,0:T(8,128)(2,1)S(1)}, bf16[80,4096]{1,0:T(8,128)(2,1)S(1)}, u32[]{:S(2)}, u32[]{:S(2)}) collective-permute-start(bf16[80,4096]{1,0:T(8,128)(2,1)S(1)} %collective-permute-done.13), channel_id=1, source_target_pairs={{0,32},{1,481},{2,34},{3,483},{4,36},{5,485},{6,38},{7,487},{8,40}... | collective-permute-start | bytes 1966088 | tf_op jit(solution)/shard_map/ppermute | solution.py:41
  102.4 14.0 %collective-permute-start.14 = (bf16[80,4096]{1,0:T(8,128)(2,1)S(1)}, bf16[80,4096]{1,0:T(8,128)(2,1)S(1)}, u32[]{:S(2)}, u32[]{:S(2)}) collective-permute-start(bf16[80,4096]{1,0:T(8,128)(2,1)S(1)} %collective-permute-done.12), channel_id=1, source_target_pairs={{0,32},{1,481},{2,34},{3,483},{4,36},{5,485},{6,38},{7,487},{8,40}... | collective-permute-start | bytes 1966088 | tf_op jit(solution)/shard_map/ppermute | solution.py:41
  109.4 10.6 %collective-permute-start.17 = (bf16[80,2048]{1,0:T(8,128)(2,1)S(1)}, bf16[80,2048]{1,0:T(8,128)(2,1)S(1)}, u32[]{:S(2)}, u32[]{:S(2)}) collective-permute-start(bf16[80,2048]{1,0:T(8,128)(2,1)S(1)} %constant_dynamic-slice_fusion.2), channel_id=1, source_target_pairs={{0,32},{1,481},{2,34},{3,483},{4,36},{5,485},{6,38},{7,487},{8,40}... | collective-permute-start | bytes 983048 | tf_op jit(solution)/shard_map/ppermute | solution.py:41
  116.5 10.2 %collective-permute-start.16 = (bf16[80,2048]{1,0:T(8,128)(2,1)S(1)}, bf16[80,2048]{1,0:T(8,128)(2,1)S(1)}, u32[]{:S(2)}, u32[]{:S(2)}) collective-permute-start(bf16[80,2048]{1,0:T(8,128)(2,1)S(1)} %constant_dynamic-slice_fusion.3), channel_id=1, source_target_pairs={{0,32},{1,481},{2,34},{3,483},{4,36},{5,485},{6,38},{7,487},{8,40}... | collective-permute-start | bytes 983048 | tf_op jit(solution)/shard_map/ppermute | solution.py:41
  127.7 15.6 %all-to-all-start = ((bf16[16,80,160]{1,2,0:T(8,128)(2,1)}), bf16[16,80,160]{1,2,0:T(8,128)(2,1)S(1)}, u32[]{:S(2)}, u32[]{:S(2)}) async-start(bf16[16,80,160]{1,2,0:T(8,128)(2,1)} %constant_dynamic-update-slice_fusion), calls=%async_computation | async-start | bytes 1310720 | tf_op jit(solution)/shard_map/all_to_all | solution.py:72
  143.7 17.1 %collective-permute-start.19 = (f32[100,128]{1,0:T(8,128)S(1)}, f32[100,128]{1,0:T(8,128)S(1)}, u32[]{:S(2)}, u32[]{:S(2)}) collective-permute-start(f32[100,128]{1,0:T(8,128)S(1)} %reshape.6), channel_id=1, source_target_pairs={{1,32},{2,64},{3,96},{4,128},{5,160},{6,192},{7,224},{8,256},{9,28... | collective-permute-start | bytes 153608 | tf_op jit(solution)/shard_map/ppermute | solution.py:82
  153.3 7.6 %collective-permute-start.18 = (f32[80,80]{0,1:T(8,128)S(1)}, f32[80,80]{0,1:T(8,128)S(1)}, u32[]{:S(2)}, u32[]{:S(2)}) collective-permute-start(f32[80,80]{0,1:T(8,128)S(1)} %get-tuple-element.8), channel_id=1, source_target_pairs={{0,16},{16,0},{32,48},{48,32},{64,80},{80,64},{96,112},{112,96},{1... | collective-permute-start | bytes 76808 | tf_op jit(solution)/shard_map/ppermute | solution.py:85

commit v5 on v4

--- a/solution.py
+++ b/solution.py
@@ -5,7 +5,6 @@
 
 AXES = ("ex", "par")
 CHUNKS = 2
-LANES = 128
 
 
 def tile_of(rows_a, rows_b):
@@ -78,8 +77,7 @@
         for p in range(par_size)
         if p != z
     ]
-    packed = total.reshape(rows * 2 * rows // LANES, LANES)
-    added = lax.ppermute(packed, AXES, mirror).reshape(rows, 2 * rows)
+    added = lax.ppermute(total, AXES, mirror)
     away = lax.dynamic_slice_in_dim(total, (1 - member) * rows, rows, 1)
     kept = lax.dynamic_slice_in_dim(total, member * rows, rows, 1)
     got = lax.ppermute(away, "ex", swap)

time: 162 us -> 164 us (1.012)
  the two profiles are of different devices: /device:TPU:16 before, /device:TPU:31 now
where the time goes in v5:
time: 164 us
  starting transfers between devices  104 us (63%)
  waiting for transfers between devices  37.5 us (23%)
  matrix products  15.1 us (9%)
  local copies, waits for them, and re-layouts  4 us (2%)
  other arithmetic  1.99 us (1%)
    ppermute x16, starting transfers between devices, hop(): return lax.ppermute(block, AXES, onward)  82.4 us
    dot_general x18, matrix products, tile_of(): lax.dot_general(rows_a, rows_b, (((1,), (1,)), ((), ())), preferred_eleme...  15.1 us
    ppermute x16, waiting for transfers between devices, hop(): return lax.ppermute(block, AXES, onward)  11.7 us
    all_to_all x1, waiting for transfers between devices, shards(): lax.all_to_all(strip, AXES, 0, 0, axis_index_groups=groups, tiled=True)  8.95 us
    ppermute x1, waiting for transfers between devices, shards(): added = lax.ppermute(total, AXES, mirror)  8.86 us
    all_to_all x1, starting transfers between devices, shards(): lax.all_to_all(strip, AXES, 0, 0, axis_index_groups=groups, tiled=True)  8.11 us
    ppermute x2, starting transfers between devices, shards(): own = [in_order(block, lax.ppermute(block, 'ex', swap)) for block in mine]  5.91 us
    ppermute x1, starting transfers between devices, shards(): added = lax.ppermute(total, AXES, mirror)  4.59 us
  transfers between devices with their start and end apart: 21, of which 14 were waited for; matrix products, arithmetic and copies ran while one was open for 11% of the time, Pallas kernels for 0%

profile of v5, /device:TPU:31, one launch (start us, length us, event | category | flops | bytes accessed | tf_op | source)
XLA Modules:
  0.0 163.6 jit_solution(9451372000133788363)
XLA Ops:
  1.4 11.1 %collective-permute-start.3 = (bf16[80,4096]{1,0:T(8,128)(2,1)S(1)}, bf16[80,4096]{1,0:T(8,128)(2,1)S(1)}, u32[]{:S(2)}, u32[]{:S(2)}) collective-permute-start(bf16[80,4096]{1,0:T(8,128)(2,1)S(1)} %get-tuple-element.6), channel_id=1, source_target_pairs={{0,32},{1,481},{2,34},{3,483},{4,36},{5,485},{6,38},{7,487},{8,40}... | collective-permute-start | bytes 1966088 | tf_op jit(solution)/shard_map/ppermute | solution.py:40
  12.5 2.6 %collective-permute-start.2 = (bf16[80,4096]{1,0:T(8,128)(2,1)S(1)}, bf16[80,4096]{1,0:T(8,128)(2,1)}, u32[]{:S(2)}, u32[]{:S(2)}) collective-permute-start(bf16[80,4096]{1,0:T(8,128)(2,1)S(1)} %get-tuple-element.5), channel_id=1, source_target_pairs={{0,32},{1,481},{2,34},{3,483},{4,36},{5,485},{6,38},{7,487},{8,40}... | collective-permute-start | bytes 1966088 | tf_op jit(solution)/shard_map/ppermute | solution.py:40
  15.2 3.0 %collective-permute-start.1 = (bf16[80,4096]{1,0:T(8,128)(2,1)S(1)}, bf16[80,4096]{1,0:T(8,128)(2,1)}, u32[]{:S(2)}, u32[]{:S(2)}) collective-permute-start(bf16[80,4096]{1,0:T(8,128)(2,1)S(1)} %get-tuple-element.6), channel_id=1, source_target_pairs={{0,16},{16,0},{32,48},{48,32},{64,80},{80,64},{96,112},{112,96},{1... | collective-permute-start | bytes 1966088 | tf_op jit(solution)/shard_map/ppermute | solution.py:54
  18.2 1.8 %collective-permute-done.3 = bf16[80,4096]{1,0:T(8,128)(2,1)S(1)} collective-permute-done((bf16[80,4096]{1,0:T(8,128)(2,1)S(1)}, bf16[80,4096]{1,0:T(8,128)(2,1)S(1)}, u32[]{:S(2)}, u32[]{:S(2)}) %collective-permute-start.3) | collective-permute-done | bytes 655392 | tf_op jit(solution)/shard_map/ppermute | solution.py:40
  20.0 5.4 %collective-permute-start.5 = (bf16[80,4096]{1,0:T(8,128)(2,1)S(1)}, bf16[80,4096]{1,0:T(8,128)(2,1)S(1)}, u32[]{:S(2)}, u32[]{:S(2)}) collective-permute-start(bf16[80,4096]{1,0:T(8,128)(2,1)S(1)} %collective-permute-done.3), channel_id=1, source_target_pairs={{0,32},{1,481},{2,34},{3,483},{4,36},{5,485},{6,38},{7,487},{8,40}... | collective-permute-start | bytes 1966088 | tf_op jit(solution)/shard_map/ppermute | solution.py:40
  25.5 2.9 %collective-permute-start = (bf16[80,4096]{1,0:T(8,128)(2,1)S(1)}, bf16[80,4096]{1,0:T(8,128)(2,1)S(1)}, u32[]{:S(2)}, u32[]{:S(2)}) collective-permute-start(bf16[80,4096]{1,0:T(8,128)(2,1)S(1)} %get-tuple-element.5), channel_id=1, source_target_pairs={{0,16},{16,0},{32,48},{48,32},{64,80},{80,64},{96,112},{112,96},{1... | collective-permute-start | bytes 1966088 | tf_op jit(solution)/shard_map/ppermute | solution.py:54
  28.9 3.6 %collective-permute-start.4 = (bf16[80,4096]{1,0:T(8,128)(2,1)}, bf16[80,4096]{1,0:T(8,128)(2,1)S(1)}, u32[]{:S(2)}, u32[]{:S(2)}) collective-permute-start(bf16[80,4096]{1,0:T(8,128)(2,1)} %collective-permute-done.2), channel_id=1, source_target_pairs={{0,32},{1,481},{2,34},{3,483},{4,36},{5,485},{6,38},{7,487},{8,40}... | collective-permute-start | bytes 1966088 | tf_op jit(solution)/shard_map/ppermute | solution.py:40
  32.5 1.6 maximum_select_fusion.1
  34.1 5.6 %collective-permute-start.7 = (bf16[80,4096]{1,0:T(8,128)(2,1)S(1)}, bf16[80,4096]{1,0:T(8,128)(2,1)S(1)}, u32[]{:S(2)}, u32[]{:S(2)}) collective-permute-start(bf16[80,4096]{1,0:T(8,128)(2,1)S(1)} %collective-permute-done.5), channel_id=1, source_target_pairs={{0,32},{1,481},{2,34},{3,483},{4,36},{5,485},{6,38},{7,487},{8,40}... | collective-permute-start | bytes 1966088 | tf_op jit(solution)/shard_map/ppermute | solution.py:40
  39.7 4.6 %collective-permute-done = bf16[80,4096]{1,0:T(8,128)(2,1)S(1)} collective-permute-done((bf16[80,4096]{1,0:T(8,128)(2,1)S(1)}, bf16[80,4096]{1,0:T(8,128)(2,1)S(1)}, u32[]{:S(2)}, u32[]{:S(2)}) %collective-permute-start) | collective-permute-done | bytes 655392 | tf_op jit(solution)/shard_map/ppermute | solution.py:54
  44.6 7.1 %collective-permute-start.6 = (bf16[80,4096]{1,0:T(8,128)(2,1)S(1)}, bf16[80,4096]{1,0:T(8,128)(2,1)S(1)}, u32[]{:S(2)}, u32[]{:S(2)}) collective-permute-start(bf16[80,4096]{1,0:T(8,128)(2,1)S(1)} %collective-permute-done.4), channel_id=1, source_target_pairs={{0,32},{1,481},{2,34},{3,483},{4,36},{5,485},{6,38},{7,487},{8,40}... | collective-permute-start | bytes 1966088 | tf_op jit(solution)/shard_map/ppermute | solution.py:40
  54.3 2.6 %collective-permute-start.9 = (bf16[80,4096]{1,0:T(8,128)(2,1)S(1)}, bf16[80,4096]{1,0:T(8,128)(2,1)S(1)}, u32[]{:S(2)}, u32[]{:S(2)}) collective-permute-start(bf16[80,4096]{1,0:T(8,128)(2,1)S(1)} %collective-permute-done.7), channel_id=1, source_target_pairs={{0,32},{1,481},{2,34},{3,483},{4,36},{5,485},{6,38},{7,487},{8,40}... | collective-permute-start | bytes 1966088 | tf_op jit(solution)/shard_map/ppermute | solution.py:40
  57.4 1.8 %collective-permute-done.6 = bf16[80,4096]{1,0:T(8,128)(2,1)S(1)} collective-permute-done((bf16[80,4096]{1,0:T(8,128)(2,1)S(1)}, bf16[80,4096]{1,0:T(8,128)(2,1)S(1)}, u32[]{:S(2)}, u32[]{:S(2)}) %collective-permute-start.6) | collective-permute-done | bytes 655392 | tf_op jit(solution)/shard_map/ppermute | solution.py:40
  59.2 5.0 %collective-permute-start.8 = (bf16[80,4096]{1,0:T(8,128)(2,1)S(1)}, bf16[80,4096]{1,0:T(8,128)(2,1)S(1)}, u32[]{:S(2)}, u32[]{:S(2)}) collective-permute-start(bf16[80,4096]{1,0:T(8,128)(2,1)S(1)} %collective-permute-done.6), channel_id=1, source_target_pairs={{0,32},{1,481},{2,34},{3,483},{4,36},{5,485},{6,38},{7,487},{8,40}... | collective-permute-start | bytes 1966088 | tf_op jit(solution)/shard_map/ppermute | solution.py:40
  64.2 2.2 %fusion.23 = bf16[16,80,160]{1,2,0:T(8,128)(2,1)} fusion(bf16[16,80,160]{1,2,0:T(8,128)(2,1)} %fusion.25, s32[]{:T(128)S(6)} %select_n.200, f32[160,80]{1,0:T(8,128)S(1)} %fusion.37, bf16[80,4096]{1,0:T(8,128)(2,1)} %collective-permute-done.2, bf16[80,4096]{1,0:T(8,128)(2,1)S(1)} %collective-permute-done, bf16[80,4096]{1,0:T(8,128)(2,1)S(1)} %get-tuple-element.5, ...), kind=kOutput, calls=%fused_computation.35 | convolution fusion | flops 110781440 | bytes 2058245 | tf_op jit(solution)/shard_map/dot_general | solution.py:11
  67.0 4.3 %collective-permute-start.11 = (bf16[80,4096]{1,0:T(8,128)(2,1)S(1)}, bf16[80,4096]{1,0:T(8,128)(2,1)S(1)}, u32[]{:S(2)}, u32[]{:S(2)}) collective-permute-start(bf16[80,4096]{1,0:T(8,128)(2,1)S(1)} %collective-permute-done.9), channel_id=1, source_target_pairs={{0,32},{1,481},{2,34},{3,483},{4,36},{5,485},{6,38},{7,487},{8,40}... | collective-permute-start | bytes 1966088 | tf_op jit(solution)/shard_map/ppermute | solution.py:40
  73.3 5.0 %collective-permute-start.10 = (bf16[80,4096]{1,0:T(8,128)(2,1)S(1)}, bf16[80,4096]{1,0:T(8,128)(2,1)S(1)}, u32[]{:S(2)}, u32[]{:S(2)}) collective-permute-start(bf16[80,4096]{1,0:T(8,128)(2,1)S(1)} %collective-permute-done.8), channel_id=1, source_target_pairs={{0,32},{1,481},{2,34},{3,483},{4,36},{5,485},{6,38},{7,487},{8,40}... | collective-permute-start | bytes 1966088 | tf_op jit(solution)/shard_map/ppermute | solution.py:40
  80.3 5.0 %collective-permute-start.13 = (bf16[80,4096]{1,0:T(8,128)(2,1)S(1)}, bf16[80,4096]{1,0:T(8,128)(2,1)S(1)}, u32[]{:S(2)}, u32[]{:S(2)}) collective-permute-start(bf16[80,4096]{1,0:T(8,128)(2,1)S(1)} %collective-permute-done.11), channel_id=1, source_target_pairs={{0,32},{1,481},{2,34},{3,483},{4,36},{5,485},{6,38},{7,487},{8,40}... | collective-permute-start | bytes 1966088 | tf_op jit(solution)/shard_map/ppermute | solution.py:40
  85.8 1.5 collective-permute-done.10
  87.3 5.0 %collective-permute-start.12 = (bf16[80,4096]{1,0:T(8,128)(2,1)S(1)}, bf16[80,4096]{1,0:T(8,128)(2,1)S(1)}, u32[]{:S(2)}, u32[]{:S(2)}) collective-permute-start(bf16[80,4096]{1,0:T(8,128)(2,1)S(1)} %collective-permute-done.10), channel_id=1, source_target_pairs={{0,32},{1,481},{2,34},{3,483},{4,36},{5,485},{6,38},{7,487},{8,40}... | collective-permute-start | bytes 1966088 | tf_op jit(solution)/shard_map/ppermute | solution.py:40
  94.3 5.0 %collective-permute-start.15 = (bf16[80,4096]{1,0:T(8,128)(2,1)S(1)}, bf16[80,4096]{1,0:T(8,128)(2,1)S(1)}, u32[]{:S(2)}, u32[]{:S(2)}) collective-permute-start(bf16[80,4096]{1,0:T(8,128)(2,1)S(1)} %collective-permute-done.13), channel_id=1, source_target_pairs={{0,32},{1,481},{2,34},{3,483},{4,36},{5,485},{6,38},{7,487},{8,40}... | collective-permute-start | bytes 1966088 | tf_op jit(solution)/shard_map/ppermute | solution.py:40
  101.4 5.0 %collective-permute-start.14 = (bf16[80,4096]{1,0:T(8,128)(2,1)S(1)}, bf16[80,4096]{1,0:T(8,128)(2,1)S(1)}, u32[]{:S(2)}, u32[]{:S(2)}) collective-permute-start(bf16[80,4096]{1,0:T(8,128)(2,1)S(1)} %collective-permute-done.12), channel_id=1, source_target_pairs={{0,32},{1,481},{2,34},{3,483},{4,36},{5,485},{6,38},{7,487},{8,40}... | collective-permute-start | bytes 1966088 | tf_op jit(solution)/shard_map/ppermute | solution.py:40
  108.4 5.0 %collective-permute-start.17 = (bf16[80,2048]{1,0:T(8,128)(2,1)S(1)}, bf16[80,2048]{1,0:T(8,128)(2,1)S(1)}, u32[]{:S(2)}, u32[]{:S(2)}) collective-permute-start(bf16[80,2048]{1,0:T(8,128)(2,1)S(1)} %constant_dynamic-slice_fusion.2), channel_id=1, source_target_pairs={{0,32},{1,481},{2,34},{3,483},{4,36},{5,485},{6,38},{7,487},{8,40}... | collective-permute-start | bytes 983048 | tf_op jit(solution)/shard_map/ppermute | solution.py:40
  113.4 2.0 %collective-permute-done.14 = bf16[80,4096]{1,0:T(8,128)(2,1)S(1)} collective-permute-done((bf16[80,4096]{1,0:T(8,128)(2,1)S(1)}, bf16[80,4096]{1,0:T(8,128)(2,1)S(1)}, u32[]{:S(2)}, u32[]{:S(2)}) %collective-permute-start.14) | collective-permute-done | bytes 655392 | tf_op jit(solution)/shard_map/ppermute | solution.py:40
  115.4 5.0 %collective-permute-start.16 = (bf16[80,2048]{1,0:T(8,128)(2,1)S(1)}, bf16[80,2048]{1,0:T(8,128)(2,1)S(1)}, u32[]{:S(2)}, u32[]{:S(2)}) collective-permute-start(bf16[80,2048]{1,0:T(8,128)(2,1)S(1)} %constant_dynamic-slice_fusion.3), channel_id=1, source_target_pairs={{0,32},{1,481},{2,34},{3,483},{4,36},{5,485},{6,38},{7,487},{8,40}... | collective-permute-start | bytes 983048 | tf_op jit(solution)/shard_map/ppermute | solution.py:40
  122.5 2.0 %collective-permute-done.16 = bf16[80,2048]{1,0:T(8,128)(2,1)S(1)} collective-permute-done((bf16[80,2048]{1,0:T(8,128)(2,1)S(1)}, bf16[80,2048]{1,0:T(8,128)(2,1)S(1)}, u32[]{:S(2)}, u32[]{:S(2)}) %collective-permute-start.16) | collective-permute-done | bytes 327712 | tf_op jit(solution)/shard_map/ppermute | solution.py:40
  125.5 8.1 %all-to-all-start = ((bf16[16,80,160]{1,2,0:T(8,128)(2,1)}), bf16[16,80,160]{1,2,0:T(8,128)(2,1)S(1)}, u32[]{:S(2)}, u32[]{:S(2)}) async-start(bf16[16,80,160]{1,2,0:T(8,128)(2,1)} %constant_dynamic-update-slice_fusion), calls=%async_computation | async-start | bytes 1310720 | tf_op jit(solution)/shard_map/all_to_all | solution.py:71
  133.7 9.0 %all-to-all-done = bf16[16,80,160]{1,2,0:T(8,128)(2,1)S(1)} async-done(((bf16[16,80,160]{1,2,0:T(8,128)(2,1)}), bf16[16,80,160]{1,2,0:T(8,128)(2,1)S(1)}, u32[]{:S(2)}, u32[]{:S(2)}) %all-to-all-start) | async-done | bytes 409632 | tf_op jit(solution)/shard_map/all_to_all | solution.py:71
  142.7 4.6 %collective-permute-start.19 = (f32[80,160]{0,1:T(8,128)S(1)}, f32[80,160]{0,1:T(8,128)S(1)}, u32[]{:S(2)}, u32[]{:S(2)}) collective-permute-start(f32[80,160]{0,1:T(8,128)S(1)} %convert_reduce_fusion), channel_id=1, source_target_pairs={{1,32},{2,64},{3,96},{4,128},{5,160},{6,192},{7,224},{8,256},{9,28... | collective-permute-start | bytes 153608 | tf_op jit(solution)/shard_map/ppermute | solution.py:80
  147.4 3.0 %collective-permute-start.18 = (f32[80,80]{1,0:T(8,128)S(1)}, f32[80,80]{1,0:T(8,128)S(1)}, u32[]{:S(2)}, u32[]{:S(2)}) collective-permute-start(f32[80,80]{1,0:T(8,128)S(1)} %copy.9), channel_id=1, source_target_pairs={{0,16},{16,0},{32,48},{48,32},{64,80},{80,64},{96,112},{112,96},{1... | collective-permute-start | bytes 76808 | tf_op jit(solution)/shard_map/ppermute | solution.py:83
  150.6 3.4 %collective-permute-done.18 = f32[80,80]{1,0:T(8,128)S(1)} collective-permute-done((f32[80,80]{1,0:T(8,128)S(1)}, f32[80,80]{1,0:T(8,128)S(1)}, u32[]{:S(2)}, u32[]{:S(2)}) %collective-permute-start.18) | collective-permute-done | bytes 25632 | tf_op jit(solution)/shard_map/ppermute | solution.py:83
  154.0 8.9 %collective-permute-done.19 = f32[80,160]{0,1:T(8,128)S(1)} collective-permute-done((f32[80,160]{0,1:T(8,128)S(1)}, f32[80,160]{0,1:T(8,128)S(1)}, u32[]{:S(2)}, u32[]{:S(2)}) %collective-permute-start.19) | collective-permute-done | bytes 51232 | tf_op jit(solution)/shard_map/ppermute | solution.py:80
  (44 shorter events, 20.0 us)
Async XLA Ops:
  1.4 18.6 %collective-permute-start.3 = (bf16[80,4096]{1,0:T(8,128)(2,1)S(1)}, bf16[80,4096]{1,0:T(8,128)(2,1)S(1)}, u32[]{:S(2)}, u32[]{:S(2)}) collective-permute-start(bf16[80,4096]{1,0:T(8,128)(2,1)S(1)} %get-tuple-element.6), channel_id=1, source_target_pairs={{0,32},{1,481},{2,34},{3,483},{4,36},{5,485},{6,38},{7,487},{8,40}... | collective-permute-start | bytes 1966088 | tf_op jit(solution)/shard_map/ppermute | solution.py:40
  12.5 16.3 %collective-permute-start.2 = (bf16[80,4096]{1,0:T(8,128)(2,1)S(1)}, bf16[80,4096]{1,0:T(8,128)(2,1)}, u32[]{:S(2)}, u32[]{:S(2)}) collective-permute-start(bf16[80,4096]{1,0:T(8,128)(2,1)S(1)} %get-tuple-element.5), channel_id=1, source_target_pairs={{0,32},{1,481},{2,34},{3,483},{4,36},{5,485},{6,38},{7,487},{8,40}... | collective-permute-start | bytes 1966088 | tf_op jit(solution)/shard_map/ppermute | solution.py:40
  15.2 17.3 %collective-permute-start.1 = (bf16[80,4096]{1,0:T(8,128)(2,1)S(1)}, bf16[80,4096]{1,0:T(8,128)(2,1)}, u32[]{:S(2)}, u32[]{:S(2)}) collective-permute-start(bf16[80,4096]{1,0:T(8,128)(2,1)S(1)} %get-tuple-element.6), channel_id=1, source_target_pairs={{0,16},{16,0},{32,48},{48,32},{64,80},{80,64},{96,112},{112,96},{1... | collective-permute-start | bytes 1966088 | tf_op jit(solution)/shard_map/ppermute | solution.py:54
  20.0 14.1 %collective-permute-start.5 = (bf16[80,4096]{1,0:T(8,128)(2,1)S(1)}, bf16[80,4096]{1,0:T(8,128)(2,1)S(1)}, u32[]{:S(2)}, u32[]{:S(2)}) collective-permute-start(bf16[80,4096]{1,0:T(8,128)(2,1)S(1)} %collective-permute-done.3), channel_id=1, source_target_pairs={{0,32},{1,481},{2,34},{3,483},{4,36},{5,485},{6,38},{7,487},{8,40}... | collective-permute-start | bytes 1966088 | tf_op jit(solution)/shard_map/ppermute | solution.py:40
  25.5 18.8 %collective-permute-start = (bf16[80,4096]{1,0:T(8,128)(2,1)S(1)}, bf16[80,4096]{1,0:T(8,128)(2,1)S(1)}, u32[]{:S(2)}, u32[]{:S(2)}) collective-permute-start(bf16[80,4096]{1,0:T(8,128)(2,1)S(1)} %get-tuple-element.5), channel_id=1, source_target_pairs={{0,16},{16,0},{32,48},{48,32},{64,80},{80,64},{96,112},{112,96},{1... | collective-permute-start | bytes 1966088 | tf_op jit(solution)/shard_map/ppermute | solution.py:54
  28.9 15.7 %collective-permute-start.4 = (bf16[80,4096]{1,0:T(8,128)(2,1)}, bf16[80,4096]{1,0:T(8,128)(2,1)S(1)}, u32[]{:S(2)}, u32[]{:S(2)}) collective-permute-start(bf16[80,4096]{1,0:T(8,128)(2,1)} %collective-permute-done.2), channel_id=1, source_target_pairs={{0,32},{1,481},{2,34},{3,483},{4,36},{5,485},{6,38},{7,487},{8,40}... | collective-permute-start | bytes 1966088 | tf_op jit(solution)/shard_map/ppermute | solution.py:40
  34.1 17.6 %copy-start = (bf16[80,8192]{1,0:T(8,128)(2,1)S(1)}, bf16[80,8192]{1,0:T(8,128)(2,1)}, u32[]{:S(2)}) copy-start(bf16[80,8192]{1,0:T(8,128)(2,1)} %param.1) | copy-start | bytes 3932164
  34.1 20.2 %collective-permute-start.7 = (bf16[80,4096]{1,0:T(8,128)(2,1)S(1)}, bf16[80,4096]{1,0:T(8,128)(2,1)S(1)}, u32[]{:S(2)}, u32[]{:S(2)}) collective-permute-start(bf16[80,4096]{1,0:T(8,128)(2,1)S(1)} %collective-permute-done.5), channel_id=1, source_target_pairs={{0,32},{1,481},{2,34},{3,483},{4,36},{5,485},{6,38},{7,487},{8,40}... | collective-permute-start | bytes 1966088 | tf_op jit(solution)/shard_map/ppermute | solution.py:40
  44.6 14.7 %collective-permute-start.6 = (bf16[80,4096]{1,0:T(8,128)(2,1)S(1)}, bf16[80,4096]{1,0:T(8,128)(2,1)S(1)}, u32[]{:S(2)}, u32[]{:S(2)}) collective-permute-start(bf16[80,4096]{1,0:T(8,128)(2,1)S(1)} %collective-permute-done.4), channel_id=1, source_target_pairs={{0,32},{1,481},{2,34},{3,483},{4,36},{5,485},{6,38},{7,487},{8,40}... | collective-permute-start | bytes 1966088 | tf_op jit(solution)/shard_map/ppermute | solution.py:40
  54.3 12.7 %collective-permute-start.9 = (bf16[80,4096]{1,0:T(8,128)(2,1)S(1)}, bf16[80,4096]{1,0:T(8,128)(2,1)S(1)}, u32[]{:S(2)}, u32[]{:S(2)}) collective-permute-start(bf16[80,4096]{1,0:T(8,128)(2,1)S(1)} %collective-permute-done.7), channel_id=1, source_target_pairs={{0,32},{1,481},{2,34},{3,483},{4,36},{5,485},{6,38},{7,487},{8,40}... | collective-permute-start | bytes 1966088 | tf_op jit(solution)/shard_map/ppermute | solution.py:40
  59.2 14.0 %collective-permute-start.8 = (bf16[80,4096]{1,0:T(8,128)(2,1)S(1)}, bf16[80,4096]{1,0:T(8,128)(2,1)S(1)}, u32[]{:S(2)}, u32[]{:S(2)}) collective-permute-start(bf16[80,4096]{1,0:T(8,128)(2,1)S(1)} %collective-permute-done.6), channel_id=1, source_target_pairs={{0,32},{1,481},{2,34},{3,483},{4,36},{5,485},{6,38},{7,487},{8,40}... | collective-permute-start | bytes 1966088 | tf_op jit(solution)/shard_map/ppermute | solution.py:40
  67.0 13.3 %collective-permute-start.11 = (bf16[80,4096]{1,0:T(8,128)(2,1)S(1)}, bf16[80,4096]{1,0:T(8,128)(2,1)S(1)}, u32[]{:S(2)}, u32[]{:S(2)}) collective-permute-start(bf16[80,4096]{1,0:T(8,128)(2,1)S(1)} %collective-permute-done.9), channel_id=1, source_target_pairs={{0,32},{1,481},{2,34},{3,483},{4,36},{5,485},{6,38},{7,487},{8,40}... | collective-permute-start | bytes 1966088 | tf_op jit(solution)/shard_map/ppermute | solution.py:40
  73.3 14.0 %collective-permute-start.10 = (bf16[80,4096]{1,0:T(8,128)(2,1)S(1)}, bf16[80,4096]{1,0:T(8,128)(2,1)S(1)}, u32[]{:S(2)}, u32[]{:S(2)}) collective-permute-start(bf16[80,4096]{1,0:T(8,128)(2,1)S(1)} %collective-permute-done.8), channel_id=1, source_target_pairs={{0,32},{1,481},{2,34},{3,483},{4,36},{5,485},{6,38},{7,487},{8,40}... | collective-permute-start | bytes 1966088 | tf_op jit(solution)/shard_map/ppermute | solution.py:40
  80.3 14.0 %collective-permute-start.13 = (bf16[80,4096]{1,0:T(8,128)(2,1)S(1)}, bf16[80,4096]{1,0:T(8,128)(2,1)S(1)}, u32[]{:S(2)}, u32[]{:S(2)}) collective-permute-start(bf16[80,4096]{1,0:T(8,128)(2,1)S(1)} %collective-permute-done.11), channel_id=1, source_target_pairs={{0,32},{1,481},{2,34},{3,483},{4,36},{5,485},{6,38},{7,487},{8,40}... | collective-permute-start | bytes 1966088 | tf_op jit(solution)/shard_map/ppermute | solution.py:40
  87.3 14.0 %collective-permute-start.12 = (bf16[80,4096]{1,0:T(8,128)(2,1)S(1)}, bf16[80,4096]{1,0:T(8,128)(2,1)S(1)}, u32[]{:S(2)}, u32[]{:S(2)}) collective-permute-start(bf16[80,4096]{1,0:T(8,128)(2,1)S(1)} %collective-permute-done.10), channel_id=1, source_target_pairs={{0,32},{1,481},{2,34},{3,483},{4,36},{5,485},{6,38},{7,487},{8,40}... | collective-permute-start | bytes 1966088 | tf_op jit(solution)/shard_map/ppermute | solution.py:40
  94.3 14.0 %collective-permute-start.15 = (bf16[80,4096]{1,0:T(8,128)(2,1)S(1)}, bf16[80,4096]{1,0:T(8,128)(2,1)S(1)}, u32[]{:S(2)}, u32[]{:S(2)}) collective-permute-start(bf16[80,4096]{1,0:T(8,128)(2,1)S(1)} %collective-permute-done.13), channel_id=1, source_target_pairs={{0,32},{1,481},{2,34},{3,483},{4,36},{5,485},{6,38},{7,487},{8,40}... | collective-permute-start | bytes 1966088 | tf_op jit(solution)/shard_map/ppermute | solution.py:40
  101.4 14.0 %collective-permute-start.14 = (bf16[80,4096]{1,0:T(8,128)(2,1)S(1)}, bf16[80,4096]{1,0:T(8,128)(2,1)S(1)}, u32[]{:S(2)}, u32[]{:S(2)}) collective-permute-start(bf16[80,4096]{1,0:T(8,128)(2,1)S(1)} %collective-permute-done.12), channel_id=1, source_target_pairs={{0,32},{1,481},{2,34},{3,483},{4,36},{5,485},{6,38},{7,487},{8,40}... | collective-permute-start | bytes 1966088 | tf_op jit(solution)/shard_map/ppermute | solution.py:40
  108.4 13.7 %collective-permute-start.17 = (bf16[80,2048]{1,0:T(8,128)(2,1)S(1)}, bf16[80,2048]{1,0:T(8,128)(2,1)S(1)}, u32[]{:S(2)}, u32[]{:S(2)}) collective-permute-start(bf16[80,2048]{1,0:T(8,128)(2,1)S(1)} %constant_dynamic-slice_fusion.2), channel_id=1, source_target_pairs={{0,32},{1,481},{2,34},{3,483},{4,36},{5,485},{6,38},{7,487},{8,40}... | collective-permute-start | bytes 983048 | tf_op jit(solution)/shard_map/ppermute | solution.py:40
  115.4 9.0 %collective-permute-start.16 = (bf16[80,2048]{1,0:T(8,128)(2,1)S(1)}, bf16[80,2048]{1,0:T(8,128)(2,1)S(1)}, u32[]{:S(2)}, u32[]{:S(2)}) collective-permute-start(bf16[80,2048]{1,0:T(8,128)(2,1)S(1)} %constant_dynamic-slice_fusion.3), channel_id=1, source_target_pairs={{0,32},{1,481},{2,34},{3,483},{4,36},{5,485},{6,38},{7,487},{8,40}... | collective-permute-start | bytes 983048 | tf_op jit(solution)/shard_map/ppermute | solution.py:40
  125.5 17.1 %all-to-all-start = ((bf16[16,80,160]{1,2,0:T(8,128)(2,1)}), bf16[16,80,160]{1,2,0:T(8,128)(2,1)S(1)}, u32[]{:S(2)}, u32[]{:S(2)}) async-start(bf16[16,80,160]{1,2,0:T(8,128)(2,1)} %constant_dynamic-update-slice_fusion), calls=%async_computation | async-start | bytes 1310720 | tf_op jit(solution)/shard_map/all_to_all | solution.py:71
  142.7 20.1 %collective-permute-start.19 = (f32[80,160]{0,1:T(8,128)S(1)}, f32[80,160]{0,1:T(8,128)S(1)}, u32[]{:S(2)}, u32[]{:S(2)}) collective-permute-start(f32[80,160]{0,1:T(8,128)S(1)} %convert_reduce_fusion), channel_id=1, source_target_pairs={{1,32},{2,64},{3,96},{4,128},{5,160},{6,192},{7,224},{8,256},{9,28... | collective-permute-start | bytes 153608 | tf_op jit(solution)/shard_map/ppermute | solution.py:80
  147.4 6.5 %collective-permute-start.18 = (f32[80,80]{1,0:T(8,128)S(1)}, f32[80,80]{1,0:T(8,128)S(1)}, u32[]{:S(2)}, u32[]{:S(2)}) collective-permute-start(f32[80,80]{1,0:T(8,128)S(1)} %copy.9), channel_id=1, source_target_pairs={{0,16},{16,0},{32,48},{48,32},{64,80},{80,64},{96,112},{112,96},{1... | collective-permute-start | bytes 76808 | tf_op jit(solution)/shard_map/ppermute | solution.py:83
